TPU v7x, 512 devices: a whole 4x8x8 slice. The times are simulated.
512 devices in a mesh: dp: 32 (over z_lo, x, core), mp: 16 (over z_hi, y).
Axes of the slice: x: 4, y: 8, z: 8 (z_hi: 2, z_lo: 4; z = z_hi * 4 + z_lo), core: 2. Of those that a mesh axis runs over, the one named last changes fastest.
Arguments:
- features: bfloat16 [4096, 8192], P('dp', 'mp'), may hold values from -110 to 110
- output_grads: bfloat16 [4096, 14336], P('dp', 'mp'), may hold values from -110 to 110
- basis: bfloat16 [8192, 512], P('dp'), may hold values from -0.0625 to 0.0625
- moment_one: float32 [8192, 14336], P('dp', 'mp'), may hold values from -4 to 4
- moment_two: float32 [8192, 14336], P('dp', 'mp'), may hold values from 0.02 to 0.5
Outputs:
- new_moment_one: float32 [8192, 14336], P('dp', 'mp')
- new_moment_two: float32 [8192, 14336], P('dp', 'mp')
- update: bfloat16 [8192, 14336], P('dp', 'mp')
All inputs are finite; a program needn't handle non-finite values.
Results may differ from a plain program's by a relative error of at most 0.001.
Values may be sent and summed in bfloat16 or wider, within the bound.
No kernel may reach another device: no remote copies, remote signals or barrier semaphores. Data moves between devices by JAX's collectives and lax.ppermute only.
A program may use at most 64 MiB of HBM per device.

v0:
```python
import jax
import jax.numpy as jnp
from jax import lax
from jax.sharding import PartitionSpec as P

D = 8192
FF = 14336


def on_device(features, output_grads, basis, moment_one, moment_two):
    every_feature = lax.all_gather(features, "mp", axis=1, tiled=True)
    tile_rows = lax.all_to_all(every_feature, "dp", split_axis=1, concat_axis=0, tiled=True)
    grad = lax.dot_general(
        tile_rows,
        lax.all_gather(output_grads, "dp", axis=0, tiled=True),
        (((0,), (0,)), ((), ())),
        preferred_element_type=jnp.float32,
    )
    basis_f = basis.astype(jnp.float32)
    partial_coeffs = jnp.dot(basis_f.T, grad, precision=lax.Precision.HIGHEST)
    coeffs = lax.psum(partial_coeffs, "dp")
    projected = grad - jnp.dot(basis_f, coeffs, precision=lax.Precision.HIGHEST)
    square_sum = lax.psum(jnp.sum(projected * projected), ("dp", "mp"))
    mean_square = square_sum / (D * FF)
    factor = jnp.minimum(1.0, lax.rsqrt(mean_square + 1e-06))
    clipped = factor * projected
    new_one = 0.9 * moment_one + 0.1 * clipped
    new_two = 0.95 * moment_two + 0.05 * clipped * clipped
    update = (new_one / (jnp.sqrt(new_two) + 1e-08)).astype(jnp.bfloat16)
    return (new_one, new_two, update)


def solution(mesh):
    in_specs = (P("dp", "mp"), P("dp", "mp"), P("dp", None), P("dp", "mp"), P("dp", "mp"))
    out_specs = (P("dp", "mp"), P("dp", "mp"), P("dp", "mp"))
    return jax.shard_map(
        on_device, mesh=mesh, in_specs=in_specs, out_specs=out_specs, check_vma=False
    )
```

profile of v0, /device:TPU:1, one launch (start us, length us, event | category | flops | bytes accessed | tf_op | source)
XLA Modules:
  0.0 623.3 jit_solution(16831306277811305279)
XLA Ops:
  7.2 0.0 copy-start
  7.2 0.0 all-gather.3.cloned.1.call-start
  7.2 1.7 copy.10
  8.9 0.0 all-gather.3.cloned.1.call-update
  8.9 0.0 all-gather.5.cloned.1.call-start
  9.0 0.7 all-gather.5.cloned.1.call-update
  9.7 0.0 all-reduce.2.cloned.1.call-start
  9.7 110.1 %all-gather.3.cloned.1.call-done = bf16[128,8192]{0,1:T(8,128)(2,1)} async-done(((bf16[128,512]{0,1:T(8,128)(2,1)}), bf16[128,8192]{0,1:T(8,128)(2,1)}) %all-gather.3.cloned.1.call-update) | async-done | bytes 2097168 | tf_op jit(solution)/shard_map/all_gather | solution.py:11
  119.9 76.5 %all_to_all.19 = bf16[128,32,256]{0,2,1:T(8,128)(2,1)} all-to-all(bf16[128,32,256]{0,2,1:T(8,128)(2,1)} %bitcast.17), channel_id=1, replica_groups=mesh['dp'=32,'mp'=16] {'dp'}, dimensions={1} | all-to-all | bytes 4194304 | tf_op jit(solution)/shard_map/all_to_all | solution.py:12
  196.4 3.3 copy.11
  199.7 22.3 %all-gather.5.cloned.1.call-done = bf16[4096,896]{1,0:T(8,128)(2,1)} async-done(((bf16[128,896]{1,0:T(8,128)(2,1)}), bf16[4096,896]{1,0:T(8,128)(2,1)}) %all-gather.5.cloned.1.call-update) | async-done | bytes 7340048 | tf_op jit(solution)/shard_map/all_gather | solution.py:15
  222.0 5.4 fusion.3
  227.4 0.0 copy-done
  227.5 2.1 convolution_bitcast_fusion
  229.6 0.0 all-reduce.2.cloned.1.call-update
  229.6 0.0 copy-start.1
  229.6 280.7 %all-reduce.2.cloned.1.call-done = f32[512,896]{0,1:T(8,128)} async-done(((f32[512,896]{0,1:T(8,128)}), f32[512,896]{0,1:T(8,128)}) %all-reduce.2.cloned.1.call-update) | async-done | bytes 1835024 | tf_op jit(solution)/shard_map/psum | solution.py:21
  510.3 3.3 multiply_reduce_fusion
  513.6 99.7 %psum.15 = f32[]{:T(128)} all-reduce(f32[]{:T(128)} %get-tuple-element.6), channel_id=1, replica_groups=mesh['dp'=32,'mp'=16] {'dp','mp'}, use_global_device_ids=true, to_apply=%region_2.0 | all-reduce | flops 1 | bytes 8 | tf_op jit(solution)/shard_map/psum | solution.py:23
  614.0 0.0 copy-done.1
  614.0 2.8 divide_convert_fusion
Async XLA Ops:
  7.2 220.3 %copy-start = (bf16[256,512]{1,0:T(8,128)(2,1)S(1)}, bf16[256,512]{1,0:T(8,128)(2,1)}, u32[]{:S(2)}) copy-start(bf16[256,512]{1,0:T(8,128)(2,1)} %param.7) | copy-start | bytes 786436
  7.2 112.7 %all-gather.3.cloned.1.call-start = ((), (), s32[]{:S(2)}) async-start(), calls=%async_computation.1 | async-start | bytes 2228224 | tf_op jit(solution)/shard_map/all_gather | solution.py:11
  8.9 213.1 %all-gather.5.cloned.1.call-start = ((), (), s32[]{:S(2)}) async-start(), calls=%async_computation.2 | async-start | bytes 7569408 | tf_op jit(solution)/shard_map/all_gather | solution.py:15
  9.7 500.6 %all-reduce.2.cloned.1.call-start = ((), (), s32[]{:S(2)}) async-start(), calls=%async_computation.3 | async-start | bytes 3670016 | tf_op jit(solution)/shard_map/psum | solution.py:21
  229.6 384.3 %copy-start.1 = (f32[256,896]{1,0:T(8,128)S(1)}, f32[256,896]{1,0:T(8,128)}, u32[]{:S(2)}) copy-start(f32[256,896]{1,0:T(8,128)} %param.9) | copy-start | bytes 2752516
Sparse Core Ops, SparseCore 0:
  11.8 108.0 all-gather.2
  122.0 99.9 all-gather.4
  229.8 280.5 all-reduce.1
where the time goes:
time: 624 us; the launch traced here: 623 us
  waiting for transfers between devices  414 us (66%)
  blocking collectives  176 us (28%)
  between operations  14.5 us (2%)
  matrix products  10.9 us (2%)
    psum x1, waiting for transfers between devices, on_device(): coeffs = lax.psum(partial_coeffs, 'dp')  281 us
    all_gather x1, waiting for transfers between devices, on_device(): every_feature = lax.all_gather(features, 'mp', axis=1, tiled=True)  110 us
    psum x1, blocking collectives, on_device(): square_sum = lax.psum(jnp.sum(projected * projected), ('dp', 'mp'))  99.7 us
    all_to_all x1, blocking collectives, on_device(): lax.all_to_all(every_feature, 'dp', split_axis=1, concat_axis=0, tiled=True)  76.5 us
    all_gather x1, waiting for transfers between devices, on_device(): lax.all_gather(output_grads, 'dp', axis=0, tiled=True)  22.3 us
  transfers between devices with their start and end apart: 3, of which 3 were waited for; matrix products, arithmetic and copies ran while one was open for 1% of the time, Pallas kernels for 0%

commit v1 on v0

v1 whole, which is shorter than its diff:
```python
import jax
import jax.numpy as jnp
from jax import lax
from jax.experimental import pallas as pl
from jax.experimental.pallas import tpu as pltpu
from jax.sharding import Mesh, PartitionSpec as P

D = 8192
FF = 14336
ZL, X, C, ZH, Y = 4, 4, 2, 2, 8
AXES = ("zl", "x", "c", "zh", "y")
DP = ("zl", "x", "c")
MP = ("zh", "y")
Q = ("zl", "x")
f32 = jnp.float32
bf16 = jnp.bfloat16


def move(value, to):
    def index(zl, x, c, zh, y):
        return (((zl * X + x) * C + c) * ZH + zh) * Y + y

    pairs = [
        (index(zl, x, c, zh, y), index(*to(zl, x, c, zh, y)))
        for zl in range(ZL)
        for x in range(X)
        for c in range(C)
        for zh in range(ZH)
        for y in range(Y)
    ]
    return lax.ppermute(value, AXES, pairs)


def transpose_place(zl, x, c, zh, y):
    q, j = X * zl + x, Y * zh + y
    return j // X, j % X, c, q // Y, q % Y


def along_y(value, step):
    return move(value, lambda zl, x, c, zh, y: (zl, x, c, zh, (y + step) % Y))


def other_core(value):
    return move(value, lambda zl, x, c, zh, y: (zl, x, 1 - c, zh, y))


def other_half(value):
    return move(value, lambda zl, x, c, zh, y: (zl, x, c, 1 - zh, y))


def spread(value, axes, n):
    copies = jnp.broadcast_to(value[None], (n,) + value.shape)
    return lax.all_to_all(copies, axes, 0, 0, tiled=True)


def parts(value, n):
    out = []
    for _ in range(n - 1):
        top = lax.reduce_precision(value, 8, 7)
        out.append(top.astype(bf16))
        value = value - top
    return out + [value.astype(bf16)]


def grad_kernel(place, g_ref, *refs):
    blocks, halves, (mine, theirs) = refs[:7], refs[7:9], refs[9:]
    y, c = place[0], place[1]
    for out, core in ((theirs, 1 - c), (mine, c)):
        rows = pl.ds(pl.multiple_of(core * 256, 256), 256)
        total = None
        for k, step in enumerate((0, -1, -2, -3, 1, 2, 3, 4)):
            at = lax.rem(y + (step + Y), Y)
            g = jnp.concatenate([g_ref[0, at], g_ref[1, at]], axis=0)
            if k < 7:
                high, low = blocks[k][rows, :256], blocks[k][rows, 256:]
            else:
                high, low = halves[0][rows, :], halves[1][rows, :]
            term = jnp.dot(high, g, preferred_element_type=f32)
            term += jnp.dot(low, g, preferred_element_type=f32)
            total = term if total is None else total + term
        out[...] = total


def on_device(features, output_grads, basis, moment_one, moment_two):
    c, zh, y = lax.axis_index("c"), lax.axis_index("zh"), lax.axis_index("y")
    cotangents = lax.all_gather(output_grads, Q, axis=0, tiled=True)

    own = move(features, transpose_place)
    basis_rows = lax.all_gather(basis, "c", axis=0, tiled=True)
    far = other_half(own)
    both = jnp.concatenate([jnp.where(zh == 0, own, far), jnp.where(zh == 0, far, own)])
    both = both.T.astype(f32)

    partial = jnp.dot(own, basis_rows, preferred_element_type=f32)
    pieces = lax.all_to_all(partial.reshape(16, 8, 512), Q, 0, 0, tiled=True)
    coded = spread(jnp.sum(pieces, axis=0), ("zh",) + Q, 32).reshape(256, 512)
    away = sum(
        lax.dot_general(
            basis_rows, p, (((1,), (1,)), ((), ())), preferred_element_type=f32
        )
        for p in parts(coded, 3)
    )
    kept = jnp.concatenate(parts(both - away, 2), axis=1)

    right, left = [kept], [kept]
    for _ in range(3):
        right.append(along_y(right[-1], 1))
        left.append(along_y(left[-1], -1))
    high = along_y(right[-1][:, :256], 1)
    low = along_y(left[-1][:, 256:], -1)

    tile = jax.ShapeDtypeStruct((256, 896), f32)
    vmem = pl.BlockSpec(memory_space=pltpu.VMEM)
    mine, theirs = pl.pallas_call(
        grad_kernel,
        out_shape=(tile, tile),
        in_specs=[pl.BlockSpec(memory_space=pltpu.SMEM)] + [vmem] * 10,
        out_specs=(vmem, vmem),
        compiler_params=pltpu.CompilerParams(vmem_limit_bytes=48 * 2**20),
        cost_estimate=pl.CostEstimate(
            flops=4 * 4096 * 256 * 896, bytes_accessed=10 * 2**20, transcendentals=0
        ),
    )(
        jnp.stack([y, c]).astype(jnp.int32),
        cotangents.reshape(ZH, Y, 128, 896),
        *right,
        *left[1:],
        high,
        low,
    )
    projected = mine + other_core(theirs)

    squares = jnp.sum((projected * projected).reshape(32, 8, 7, 128), axis=(0, 2))
    squares = jnp.sum(spread(squares, DP, 32), axis=0)
    square_sum = jnp.sum(spread(squares, MP, 16))
    mean_square = square_sum / (D * FF)
    factor = jnp.minimum(1.0, lax.rsqrt(mean_square + 1e-06))
    clipped = factor * projected
    new_one = 0.9 * moment_one + 0.1 * clipped
    new_two = 0.95 * moment_two + 0.05 * clipped * clipped
    update = (new_one / (jnp.sqrt(new_two) + 1e-08)).astype(bf16)
    return (new_one, new_two, update)


def solution(mesh):
    fine = Mesh(mesh.devices.reshape(ZL, X, C, ZH, Y), AXES)
    tile = P(DP, MP)
    return jax.shard_map(
        on_device,
        mesh=fine,
        in_specs=(tile, tile, P(DP, None), tile, tile),
        out_specs=(tile, tile, tile),
        check_vma=False,
    )
```

time: 624 us -> 223 us (0.36)
  waiting for transfers between devices: 414 us -> 48.2 us
  blocking collectives: 176 us -> 78.1 us
  starting transfers between devices: 0.12 us -> 66.1 us
  matrix products: 10.9 us -> 1.26 us
  Pallas kernels: 0 us -> 6.6 us
    psum x1 -> x0, waiting for transfers between devices: 281 us -> none  [on_device(): coeffs = lax.psum(partial_coeffs, 'dp')]
    all_gather x2 -> x1, waiting for transfers between devices: 132 us -> 0.01 us  [on_device(): cotangents = lax.all_gather(output_grads, Q, axis=0, tiled=True)]
    psum x1 -> x0, blocking collectives: 99.7 us -> none  [on_device(): square_sum = lax.psum(jnp.sum(projected * projected), ('dp', 'mp'))]
    ppermute x0 -> x11, starting transfers between devices: none -> 52.6 us  [move(): return lax.ppermute(value, AXES, pairs)]
    ppermute x0 -> x11, waiting for transfers between devices: none -> 47.5 us  [move(): return lax.ppermute(value, AXES, pairs)]
    all_to_all x0 -> x1, starting transfers between devices: none -> 13.5 us  [spread(): return lax.all_to_all(copies, axes, 0, 0, tiled=True)]
    dot_general x3 -> x4, matrix products: 10.9 us -> 1.26 us  [the longest x3 1.02 us: on_device(): lax.dot_general(basis_rows, p, (((1,), (1,)), ((), ())), preferred_elemen...]
    all_gather x0 -> x1, blocking collectives: none -> 8.9 us  [on_device(): basis_rows = lax.all_gather(basis, 'c', axis=0, tiled=True)]
  transfers between devices with their start and end apart: 3 -> 13, of which waited for: 3 -> 7; matrix products, arithmetic and copies ran while one was open for 1% -> 2% of each run, Pallas kernels for 0% -> 0%
where the time goes in v1:
time: 223 us; the launch traced here: 222 us
  blocking collectives  78.1 us (35%)
  starting transfers between devices  66.1 us (30%)
  waiting for transfers between devices  48.2 us (22%)
  between operations  15 us (7%)
  Pallas kernels  6.6 us (3%)
  local copies, waits for them, and re-layouts  4.4 us (2%)
  other arithmetic  2.69 us (1%)
    ppermute x11, starting transfers between devices, move(): return lax.ppermute(value, AXES, pairs)  52.6 us
    ppermute x11, waiting for transfers between devices, move(): return lax.ppermute(value, AXES, pairs)  47.5 us
    all_to_all x1, blocking collectives, on_device(): pieces = lax.all_to_all(partial.reshape(16, 8, 512), Q, 0, 0, tiled=True)  35.5 us
    all_to_all x2, blocking collectives, spread(): return lax.all_to_all(copies, axes, 0, 0, tiled=True)  33.7 us
    all_to_all x1, starting transfers between devices, spread(): return lax.all_to_all(copies, axes, 0, 0, tiled=True)  13.5 us
    all_gather x1, blocking collectives, on_device(): basis_rows = lax.all_gather(basis, 'c', axis=0, tiled=True)  8.9 us
    pallas_call x1, Pallas kernels, on_device(): pl.pallas_call(grad_kernel, out_shape=(tile, tile), in_specs=[pl.BlockSpe...  6.6 us
  transfers between devices with their start and end apart: 13, of which 7 were waited for; matrix products, arithmetic and copies ran while one was open for 2% of the time, Pallas kernels for 0%

profile of v1, /device:TPU:1, one launch (start us, length us, event | category | flops | bytes accessed | tf_op | source)
XLA Modules:
  0.0 222.3 jit_solution(12102295848139977259)
XLA Ops:
  9.6 8.9 %all_gather.7 = bf16[512,512]{1,0:T(8,128)(2,1)S(1)} all-gather(bf16[256,512]{1,0:T(8,128)(2,1)} %param.7), channel_id=1, replica_groups=mesh['zl'=4,'x'=4,'c'=2,'zh'=2,'y'=8] {'c'}, dimensions={0}, use_global_device_ids=true | all-gather | bytes 786432 | tf_op jit(solution)/shard_map/all_gather | solution.py:89
  18.8 35.5 %all_to_all.20 = f32[16,8,512]{2,1,0:T(8,128)S(1)} all-to-all(f32[16,8,512]{2,1,0:T(8,128)S(1)} %convolution_bitcast_fusion), channel_id=1, replica_groups=mesh['zl'=4,'x'=4,'c'=2,'zh'=2,'y'=8] {'zl','x'}, dimensions={0} | all-to-all | bytes 524288 | tf_op jit(solution)/shard_map/all_to_all | solution.py:95
  55.1 13.5 %all-to-all-start.1 = ((f32[32,8,512]{2,1,0:T(8,128)}), f32[32,8,512]{2,1,0:T(8,128)S(1)}, u32[]{:S(2)}, u32[]{:S(2)}) async-start(f32[32,8,512]{2,1,0:T(8,128)} %broadcast_in_dim.6), calls=%async_computation.1 | async-start | bytes 1048576 | tf_op jit(solution)/shard_map/all_to_all | solution.py:53
  68.6 7.1 %collective-permute-start.1 = (bf16[128,512]{0,1:T(8,128)(2,1)S(1)}, bf16[128,512]{0,1:T(8,128)(2,1)S(1)}, u32[]{:S(2)}, u32[]{:S(2)}) collective-permute-start(bf16[128,512]{0,1:T(8,128)(2,1)S(1)} %collective-permute-done), channel_id=1, source_target_pairs={{0,8},{1,9},{2,10},{3,11},{4,12},{5,13},{6,14},{7,15},{8,0},{9,1},... | collective-permute-start | bytes 393224 | tf_op jit(solution)/shard_map/ppermute | solution.py:31
  75.7 19.3 %collective-permute-done.1 = bf16[128,512]{0,1:T(8,128)(2,1)S(1)} collective-permute-done((bf16[128,512]{0,1:T(8,128)(2,1)S(1)}, bf16[128,512]{0,1:T(8,128)(2,1)S(1)}, u32[]{:S(2)}, u32[]{:S(2)}) %collective-permute-start.1) | collective-permute-done | bytes 131104 | tf_op jit(solution)/shard_map/ppermute | solution.py:31
  96.0 13.2 %collective-permute-start.5 = (bf16[512,512]{1,0:T(8,128)(2,1)S(1)}, bf16[512,512]{1,0:T(8,128)(2,1)S(1)}, u32[]{:S(2)}, u32[]{:S(2)}) collective-permute-start(bf16[512,512]{1,0:T(8,128)(2,1)S(1)} %pad_maximum_fusion.refs_0_), channel_id=1, source_target_pairs={{0,7},{1,0},{2,1},{3,2},{4,3},{5,4},{6,5},{7,6},{8,15},{9,8},{10,9... | collective-permute-start | bytes 1572872 | tf_op jit(solution)/shard_map/ppermute | solution.py:31
  109.2 1.9 collective-permute-start.2
  111.2 7.4 %collective-permute-done.5.refs_4_ = bf16[512,512]{1,0:T(8,128)(2,1)S(1)} collective-permute-done((bf16[512,512]{1,0:T(8,128)(2,1)S(1)}, bf16[512,512]{1,0:T(8,128)(2,1)S(1)}, u32[]{:S(2)}, u32[]{:S(2)}) %collective-permute-start.5) | collective-permute-done | bytes 524320 | tf_op jit(solution)/shard_map/ppermute | solution.py:31
  118.6 5.3 %collective-permute-start.6 = (bf16[512,512]{1,0:T(8,128)(2,1)S(1)}, bf16[512,512]{1,0:T(8,128)(2,1)S(1)}, u32[]{:S(2)}, u32[]{:S(2)}) collective-permute-start(bf16[512,512]{1,0:T(8,128)(2,1)S(1)} %collective-permute-done.5.refs_4_), channel_id=1, source_target_pairs={{0,7},{1,0},{2,1},{3,2},{4,3},{5,4},{6,5},{7,6},{8,15},{9,8},{10,9... | collective-permute-start | bytes 1572872 | tf_op jit(solution)/shard_map/ppermute | solution.py:31
  123.9 1.9 collective-permute-start.3
  125.8 6.5 %collective-permute-done.6.refs_5_ = bf16[512,512]{1,0:T(8,128)(2,1)S(1)} collective-permute-done((bf16[512,512]{1,0:T(8,128)(2,1)S(1)}, bf16[512,512]{1,0:T(8,128)(2,1)S(1)}, u32[]{:S(2)}, u32[]{:S(2)}) %collective-permute-start.6) | collective-permute-done | bytes 524320 | tf_op jit(solution)/shard_map/ppermute | solution.py:31
  132.3 5.3 %collective-permute-start.7 = (bf16[512,512]{1,0:T(8,128)(2,1)S(1)}, bf16[512,512]{1,0:T(8,128)(2,1)S(1)}, u32[]{:S(2)}, u32[]{:S(2)}) collective-permute-start(bf16[512,512]{1,0:T(8,128)(2,1)S(1)} %collective-permute-done.6.refs_5_), channel_id=1, source_target_pairs={{0,7},{1,0},{2,1},{3,2},{4,3},{5,4},{6,5},{7,6},{8,15},{9,8},{10,9... | collective-permute-start | bytes 1572872 | tf_op jit(solution)/shard_map/ppermute | solution.py:31
  137.7 1.9 collective-permute-start.4
  139.6 5.6 %collective-permute-done.7.refs_6_ = bf16[512,512]{1,0:T(8,128)(2,1)S(1)} collective-permute-done((bf16[512,512]{1,0:T(8,128)(2,1)S(1)}, bf16[512,512]{1,0:T(8,128)(2,1)S(1)}, u32[]{:S(2)}, u32[]{:S(2)}) %collective-permute-start.7) | collective-permute-done | bytes 524320 | tf_op jit(solution)/shard_map/ppermute | solution.py:31
  145.9 5.3 %collective-permute-start.9 = (bf16[512,256]{1,0:T(8,128)(2,1)}, bf16[512,256]{1,0:T(8,128)(2,1)S(1)}, u32[]{:S(2)}, u32[]{:S(2)}) collective-permute-start(bf16[512,256]{1,0:T(8,128)(2,1)} %slice.9), channel_id=1, source_target_pairs={{0,7},{1,0},{2,1},{3,2},{4,3},{5,4},{6,5},{7,6},{8,15},{9,8},{10,9... | collective-permute-start | bytes 786440 | tf_op jit(solution)/shard_map/ppermute | solution.py:31
  152.0 1.9 collective-permute-start.8
  154.8 5.8 %collective-permute-done.8.refs_7_ = bf16[512,256]{1,0:T(8,128)(2,1)} collective-permute-done((bf16[512,256]{1,0:T(8,128)(2,1)}, bf16[512,256]{1,0:T(8,128)(2,1)}, u32[]{:S(2)}, u32[]{:S(2)}) %collective-permute-start.8) | collective-permute-done | bytes 262176 | tf_op jit(solution)/shard_map/ppermute | solution.py:31
  160.6 1.0 copy-done.1
  161.6 6.6 %shard_map.76 = (f32[256,896]{1,0:T(8,128)S(1)}, f32[256,896]{1,0:T(8,128)S(1)}) custom-call(s32[2]{0:T(128)S(1)} %pad_add_fusion.place, bf16[2,8,128,896]{3,2,1,0:T(8,128)(2,1)} %bitcast.27, bf16[512,512]{1,0:T(8,128)(2,1)S(1)} %pad_maximum_fusion.refs_0_, bf16[512,512]{1,0:T(8,128)(2,1)S(1)} %collective-permute-done.2.refs_1_, ...), custom_call_target="tpu_custom_call" | custom-call | flops 3758096384 | bytes 10485760 | tf_op jit(solution)/shard_map/pallas_call | solution.py:114
  168.3 8.1 %collective-permute-start.10 = (f32[256,896]{1,0:T(8,128)S(1)}, f32[256,896]{1,0:T(8,128)S(1)}, u32[]{:S(2)}, u32[]{:S(2)}) collective-permute-start(f32[256,896]{1,0:T(8,128)S(1)} %get-tuple-element.6), channel_id=1, source_target_pairs={{0,16},{1,17},{2,18},{3,19},{4,20},{5,21},{6,22},{7,23},{8,24},{9,... | collective-permute-start | bytes 2752520 | tf_op jit(solution)/shard_map/ppermute | solution.py:31
  176.3 2.1 collective-permute-done.10
  178.7 15.5 %all_to_all.21 = f32[32,8,128]{2,1,0:T(8,128)S(1)} all-to-all(f32[32,8,128]{2,1,0:T(8,128)S(1)} %broadcast_in_dim.7), channel_id=1, replica_groups=mesh['zl'=4,'x'=4,'c'=2,'zh'=2,'y'=8] {'zl','x','c'}, dimensions={0} | all-to-all | bytes 262144 | tf_op jit(solution)/shard_map/all_to_all | solution.py:53
  194.3 18.2 %all_to_all.22 = f32[16,8,128]{2,1,0:T(8,128)S(1)} all-to-all(f32[16,8,128]{2,1,0:T(8,128)S(1)} %broadcast_in_dim.8), channel_id=1, replica_groups=mesh['zl'=4,'x'=4,'c'=2,'zh'=2,'y'=8] {'zh','y'}, dimensions={0} | all-to-all | bytes 131072 | tf_op jit(solution)/shard_map/all_to_all | solution.py:53
  213.8 1.6 divide_convert_fusion
  (34 shorter events, 7.9 us)
Async XLA Ops:
  7.2 153.4 %all-gather.2.cloned.1.call-start = ((), (), s32[]{:S(2)}) async-start(), calls=%async_computation.4 | async-start | bytes 3899392 | tf_op jit(solution)/shard_map/all_gather | solution.py:86
  8.9 9.6 %collective-permute-start = (bf16[128,512]{0,1:T(8,128)(2,1)S(1)}, bf16[128,512]{0,1:T(8,128)(2,1)S(1)}, u32[]{:S(2)}, u32[]{:S(2)}) collective-permute-start(bf16[128,512]{0,1:T(8,128)(2,1)S(1)} %copy.12), channel_id=1, source_target_pairs={{0,0},{1,32},{2,64},{3,96},{4,128},{5,160},{6,192},{7,224},{8,256}... | collective-permute-start | bytes 393224 | tf_op jit(solution)/shard_map/ppermute | solution.py:31
  55.1 39.8 %all-to-all-start.1 = ((f32[32,8,512]{2,1,0:T(8,128)}), f32[32,8,512]{2,1,0:T(8,128)S(1)}, u32[]{:S(2)}, u32[]{:S(2)}) async-start(f32[32,8,512]{2,1,0:T(8,128)} %broadcast_in_dim.6), calls=%async_computation.1 | async-start | bytes 1048576 | tf_op jit(solution)/shard_map/all_to_all | solution.py:53
  68.6 26.3 %collective-permute-start.1 = (bf16[128,512]{0,1:T(8,128)(2,1)S(1)}, bf16[128,512]{0,1:T(8,128)(2,1)S(1)}, u32[]{:S(2)}, u32[]{:S(2)}) collective-permute-start(bf16[128,512]{0,1:T(8,128)(2,1)S(1)} %collective-permute-done), channel_id=1, source_target_pairs={{0,8},{1,9},{2,10},{3,11},{4,12},{5,13},{6,14},{7,15},{8,0},{9,1},... | collective-permute-start | bytes 393224 | tf_op jit(solution)/shard_map/ppermute | solution.py:31
  96.0 22.6 %collective-permute-start.5 = (bf16[512,512]{1,0:T(8,128)(2,1)S(1)}, bf16[512,512]{1,0:T(8,128)(2,1)S(1)}, u32[]{:S(2)}, u32[]{:S(2)}) collective-permute-start(bf16[512,512]{1,0:T(8,128)(2,1)S(1)} %pad_maximum_fusion.refs_0_), channel_id=1, source_target_pairs={{0,7},{1,0},{2,1},{3,2},{4,3},{5,4},{6,5},{7,6},{8,15},{9,8},{10,9... | collective-permute-start | bytes 1572872 | tf_op jit(solution)/shard_map/ppermute | solution.py:31
  109.2 14.7 %collective-permute-start.2 = (bf16[512,512]{1,0:T(8,128)(2,1)S(1)}, bf16[512,512]{1,0:T(8,128)(2,1)S(1)}, u32[]{:S(2)}, u32[]{:S(2)}) collective-permute-start(bf16[512,512]{1,0:T(8,128)(2,1)S(1)} %pad_maximum_fusion.refs_0_), channel_id=1, source_target_pairs={{0,1},{1,2},{2,3},{3,4},{4,5},{5,6},{6,7},{7,0},{8,9},{9,10},{10,1... | collective-permute-start | bytes 1572872 | tf_op jit(solution)/shard_map/ppermute | solution.py:31
  118.6 13.8 %collective-permute-start.6 = (bf16[512,512]{1,0:T(8,128)(2,1)S(1)}, bf16[512,512]{1,0:T(8,128)(2,1)S(1)}, u32[]{:S(2)}, u32[]{:S(2)}) collective-permute-start(bf16[512,512]{1,0:T(8,128)(2,1)S(1)} %collective-permute-done.5.refs_4_), channel_id=1, source_target_pairs={{0,7},{1,0},{2,1},{3,2},{4,3},{5,4},{6,5},{7,6},{8,15},{9,8},{10,9... | collective-permute-start | bytes 1572872 | tf_op jit(solution)/shard_map/ppermute | solution.py:31
  123.9 13.7 %collective-permute-start.3 = (bf16[512,512]{1,0:T(8,128)(2,1)S(1)}, bf16[512,512]{1,0:T(8,128)(2,1)S(1)}, u32[]{:S(2)}, u32[]{:S(2)}) collective-permute-start(bf16[512,512]{1,0:T(8,128)(2,1)S(1)} %collective-permute-done.2.refs_1_), channel_id=1, source_target_pairs={{0,1},{1,2},{2,3},{3,4},{4,5},{5,6},{6,7},{7,0},{8,9},{9,10},{10,1... | collective-permute-start | bytes 1572872 | tf_op jit(solution)/shard_map/ppermute | solution.py:31
  132.3 12.8 %collective-permute-start.7 = (bf16[512,512]{1,0:T(8,128)(2,1)S(1)}, bf16[512,512]{1,0:T(8,128)(2,1)S(1)}, u32[]{:S(2)}, u32[]{:S(2)}) collective-permute-start(bf16[512,512]{1,0:T(8,128)(2,1)S(1)} %collective-permute-done.6.refs_5_), channel_id=1, source_target_pairs={{0,7},{1,0},{2,1},{3,2},{4,3},{5,4},{6,5},{7,6},{8,15},{9,8},{10,9... | collective-permute-start | bytes 1572872 | tf_op jit(solution)/shard_map/ppermute | solution.py:31
  137.7 13.6 %copy-start = (bf16[512,512]{1,0:T(8,128)(2,1)}, bf16[512,512]{1,0:T(8,128)(2,1)S(1)}, u32[]{:S(2)}) copy-start(bf16[512,512]{1,0:T(8,128)(2,1)S(1)} %collective-permute-done.3.refs_2_) | copy-start | bytes 1572868
  137.7 13.5 %collective-permute-start.4 = (bf16[512,512]{1,0:T(8,128)(2,1)S(1)}, bf16[512,512]{1,0:T(8,128)(2,1)S(1)}, u32[]{:S(2)}, u32[]{:S(2)}) collective-permute-start(bf16[512,512]{1,0:T(8,128)(2,1)S(1)} %collective-permute-done.3.refs_2_), channel_id=1, source_target_pairs={{0,1},{1,2},{2,3},{3,4},{4,5},{5,6},{6,7},{7,0},{8,9},{9,10},{10,1... | collective-permute-start | bytes 1572872 | tf_op jit(solution)/shard_map/ppermute | solution.py:31
  145.9 8.9 %collective-permute-start.9 = (bf16[512,256]{1,0:T(8,128)(2,1)}, bf16[512,256]{1,0:T(8,128)(2,1)S(1)}, u32[]{:S(2)}, u32[]{:S(2)}) collective-permute-start(bf16[512,256]{1,0:T(8,128)(2,1)} %slice.9), channel_id=1, source_target_pairs={{0,7},{1,0},{2,1},{3,2},{4,3},{5,4},{6,5},{7,6},{8,15},{9,8},{10,9... | collective-permute-start | bytes 786440 | tf_op jit(solution)/shard_map/ppermute | solution.py:31
  152.0 8.6 %collective-permute-start.8 = (bf16[512,256]{1,0:T(8,128)(2,1)}, bf16[512,256]{1,0:T(8,128)(2,1)}, u32[]{:S(2)}, u32[]{:S(2)}) collective-permute-start(bf16[512,256]{1,0:T(8,128)(2,1)} %slice.8), channel_id=1, source_target_pairs={{0,1},{1,2},{2,3},{3,4},{4,5},{5,6},{6,7},{7,0},{8,9},{9,10},{10,1... | collective-permute-start | bytes 786440 | tf_op jit(solution)/shard_map/ppermute | solution.py:31
  160.6 1.0 copy-start.1
  168.2 45.5 %copy-start.2 = (f32[256,896]{1,0:T(8,128)S(1)}, f32[256,896]{1,0:T(8,128)}, u32[]{:S(2)}) copy-start(f32[256,896]{1,0:T(8,128)} %param.9) | copy-start | bytes 2752516
  168.3 45.5 %copy-start.3 = (f32[256,896]{1,0:T(8,128)S(1)}, f32[256,896]{1,0:T(8,128)}, u32[]{:S(2)}) copy-start(f32[256,896]{1,0:T(8,128)} %param.8) | copy-start | bytes 2752516
  168.3 10.2 %collective-permute-start.10 = (f32[256,896]{1,0:T(8,128)S(1)}, f32[256,896]{1,0:T(8,128)S(1)}, u32[]{:S(2)}, u32[]{:S(2)}) collective-permute-start(f32[256,896]{1,0:T(8,128)S(1)} %get-tuple-element.6), channel_id=1, source_target_pairs={{0,16},{1,17},{2,18},{3,19},{4,20},{5,21},{6,22},{7,23},{8,24},{9,... | collective-permute-start | bytes 2752520 | tf_op jit(solution)/shard_map/ppermute | solution.py:31
Sparse Core Ops, SparseCore 0:
  10.1 100.6 all-gather.1

commit v2 on v1

v2 whole, which is shorter than its diff:
```python
import functools

import jax
import jax.numpy as jnp
from jax import lax
from jax.experimental import pallas as pl
from jax.experimental.pallas import tpu as pltpu
from jax.sharding import Mesh, PartitionSpec as P

D = 8192
FF = 14336
ZL, X, C, ZH, Y = 4, 4, 2, 2, 8
AXES = ("zl", "x", "c", "zh", "y")
DP = ("zl", "x", "c")
MP = ("zh", "y")
Q = ("zl", "x")
f32 = jnp.float32
bf16 = jnp.bfloat16
f16 = jnp.float16


def move(value, to):
    def index(zl, x, c, zh, y):
        return (((zl * X + x) * C + c) * ZH + zh) * Y + y

    pairs = [
        (index(zl, x, c, zh, y), index(*to(zl, x, c, zh, y)))
        for zl in range(ZL)
        for x in range(X)
        for c in range(C)
        for zh in range(ZH)
        for y in range(Y)
    ]
    return lax.ppermute(value, AXES, pairs)


def transpose_place(zl, x, c, zh, y):
    q, j = X * zl + x, Y * zh + y
    return j // X, j % X, c, q // Y, q % Y


def along_y(value, step):
    return move(value, lambda zl, x, c, zh, y: (zl, x, c, zh, (y + step) % Y))


def other_core(value):
    return move(value, lambda zl, x, c, zh, y: (zl, x, 1 - c, zh, y))


def other_half(value):
    return move(value, lambda zl, x, c, zh, y: (zl, x, c, 1 - zh, y))


def spread(value, axes, n):
    copies = jnp.broadcast_to(value[None], (n,) + value.shape)
    return lax.all_to_all(copies, axes, 0, 0, tiled=True)


def parts(value, n):
    out = []
    for _ in range(n - 1):
        top = lax.reduce_precision(value, 8, 7)
        out.append(top.astype(bf16))
        value = value - top
    return out + [value.astype(bf16)]


def code(value):
    largest = jnp.max(jnp.abs(value), axis=0, keepdims=True)
    scale = lax.reduce_precision(jnp.maximum(largest, 1.0) * 2.0**-14, 5, 10)
    rows = jnp.broadcast_to(scale, (16, value.shape[1]))
    return jnp.concatenate([(value / scale).astype(f16), rows.astype(f16)])


def decode(block):
    value = block[:512].astype(f32) * block[512:513].astype(f32)
    return parts(value, 2)


def near_kernel(steps, place, g_ref, *refs):
    n = len(steps)
    blocks, rest = refs[: 2 * n], refs[2 * n :]
    total, out = rest if len(rest) == 2 else (None, rest[0])
    value = None if total is None else total[...]
    for k, step in enumerate(steps):
        at = lax.rem(place[0] + (step + Y), Y)
        g = jnp.concatenate([g_ref[0, at], g_ref[1, at]], axis=0)
        for block in blocks[2 * k : 2 * k + 2]:
            term = jnp.dot(block[...], g, preferred_element_type=f32)
            value = term if value is None else value + term
    out[...] = value


def last_kernel(place, g_ref, high, low, total, out):
    rows = pl.ds(pl.multiple_of(place[0] * 256, 256), 256)
    value = total[rows, :]
    for block in (high, low):
        value += jnp.dot(block[rows, :], g_ref[...], preferred_element_type=f32)
    out[...] = value


def call(kernel, place, given, count, products):
    vmem = pl.BlockSpec(memory_space=pltpu.VMEM)
    return pl.pallas_call(
        kernel,
        out_shape=jax.ShapeDtypeStruct((count, 896), f32),
        in_specs=[pl.BlockSpec(memory_space=pltpu.SMEM)] + [vmem] * len(given),
        out_specs=vmem,
        compiler_params=pltpu.CompilerParams(vmem_limit_bytes=40 * 2**20),
        cost_estimate=pl.CostEstimate(
            flops=2 * products * 256 * count * 896,
            bytes_accessed=2**20 * products,
            transcendentals=0,
        ),
    )(place.astype(jnp.int32).reshape(1), *given)


def on_device(features, output_grads, basis, moment_one, moment_two):
    c, zh, y = lax.axis_index("c"), lax.axis_index("zh"), lax.axis_index("y")
    cotangents = lax.all_gather(output_grads, Q, axis=0, tiled=True)
    g = cotangents.reshape(ZH, Y, 128, 896)

    own = move(features, transpose_place)
    far = other_half(own)
    basis_rows = lax.all_gather(basis, "c", axis=0, tiled=True)

    partial = jnp.dot(own, basis_rows, preferred_element_type=f32)
    pieces = lax.all_to_all(partial.reshape(16, 8, 512), Q, 0, 0, tiled=True)
    summed, own, far = lax.optimization_barrier((jnp.sum(pieces, axis=0), own, far))
    both = jnp.concatenate([jnp.where(zh == 0, own, far), jnp.where(zh == 0, far, own)])
    both = both.T.astype(f32)
    coded = spread(summed, ("zh",) + Q, 32).reshape(256, 512)
    away = sum(
        lax.dot_general(
            basis_rows, p, (((1,), (1,)), ((), ())), preferred_element_type=f32
        )
        for p in parts(coded, 3)
    )
    kept = code(both - away)

    right, left = [kept], [kept]
    for _ in range(3):
        right.append(along_y(right[-1], 1))
        left.append(along_y(left[-1], -1))

    near = decode(right[0])
    for s in (1, 2):
        near += decode(right[s]) + decode(left[s])
    total = call(
        functools.partial(near_kernel, (0, -1, 1, -2, 2)), y, [g, *near], 512, 10
    )
    total, right[3], left[3] = lax.optimization_barrier((total, right[3], left[3]))
    across = [along_y(right[3][:, :128], 1), along_y(left[3][:, 128:], -1)]
    third = decode(right[3]) + decode(left[3])
    total = call(
        functools.partial(near_kernel, (-3, 3)), y, [g, *third, total], 512, 4
    )
    g_last = lax.dynamic_index_in_dim(g, lax.rem(y + 4, Y), 1, False).reshape(256, 896)
    last = [decode(half) for half in across]
    last = [jnp.concatenate(pair, axis=1) for pair in zip(*last)]
    received = other_core(call(last_kernel, 1 - c, [g_last, *last, total], 256, 2))
    projected = call(last_kernel, c, [g_last, *last, total], 256, 2) + received

    squares = jnp.sum((projected * projected).reshape(256, 7, 128), axis=(0, 1))
    squares = jnp.sum(spread(squares[None], ("x", "c", "y"), 64), axis=0)
    square_sum = jnp.sum(spread(squares, ("zh", "zl"), 8))
    mean_square = square_sum / (D * FF)
    factor = jnp.minimum(1.0, lax.rsqrt(mean_square + 1e-06))
    clipped = factor * projected
    new_one = 0.9 * moment_one + 0.1 * clipped
    new_two = 0.95 * moment_two + 0.05 * clipped * clipped
    update = (new_one / (jnp.sqrt(new_two) + 1e-08)).astype(bf16)
    return (new_one, new_two, update)


def solution(mesh):
    fine = Mesh(mesh.devices.reshape(ZL, X, C, ZH, Y), AXES)
    tile = P(DP, MP)
    return jax.shard_map(
        on_device,
        mesh=fine,
        in_specs=(tile, tile, P(DP, None), tile, tile),
        out_specs=(tile, tile, tile),
        check_vma=False,
    )
```

time: 223 us -> 203 us (0.910)
  blocking collectives: 78.1 us -> 36.5 us
  starting transfers between devices: 66.1 us -> 95.6 us
  waiting for transfers between devices: 48.2 us -> 38.4 us
  other arithmetic: 2.69 us -> 5.16 us
    all_to_all x1 -> x0, blocking collectives: 35.5 us -> none  [on_device(): pieces = lax.all_to_all(partial.reshape(16, 8, 512), Q, 0, 0, tiled=True)]
    ppermute x11, waiting for transfers between devices: 47.5 us -> 15.9 us  [move(): return lax.ppermute(value, AXES, pairs)]
    all_to_all x0 -> x1, starting transfers between devices: none -> 26.7 us  [on_device(): pieces = lax.all_to_all(partial.reshape(16, 8, 512), Q, 0, 0, tiled=True)]
    all_to_all x1, waiting for transfers between devices: 0.01 us -> 21.7 us  [spread(): return lax.all_to_all(copies, axes, 0, 0, tiled=True)]
    all_to_all x2, blocking collectives: 33.7 us -> 27.6 us  [spread(): return lax.all_to_all(copies, axes, 0, 0, tiled=True)]
    all_to_all x1, starting transfers between devices: 13.5 us -> 19.1 us  [spread(): return lax.all_to_all(copies, axes, 0, 0, tiled=True)]
    ppermute x11, starting transfers between devices: 52.6 us -> 49.8 us  [move(): return lax.ppermute(value, AXES, pairs)]
    pallas_call x1 -> x4, Pallas kernels: 6.6 us -> 5 us  [call(): pl.pallas_call(kernel, out_shape=jax.ShapeDtypeStruct((count, 896), f32),...]
  transfers between devices with their start and end apart: 13 -> 14, of which waited for: 7 -> 6; matrix products, arithmetic and copies ran while one was open for 2% -> 3% of each run, Pallas kernels for 0% -> 2%
where the time goes in v2:
time: 203 us; the launch traced here: 202 us
  starting transfers between devices  95.6 us (47%)
  waiting for transfers between devices  38.4 us (19%)
  blocking collectives  36.5 us (18%)
  between operations  15.1 us (7%)
  other arithmetic  5.16 us (3%)
  Pallas kernels  5 us (2%)
  local copies, waits for them, and re-layouts  4.06 us (2%)
    ppermute x11, starting transfers between devices, move(): return lax.ppermute(value, AXES, pairs)  49.8 us
    all_to_all x2, blocking collectives, spread(): return lax.all_to_all(copies, axes, 0, 0, tiled=True)  27.6 us
    all_to_all x1, starting transfers between devices, on_device(): pieces = lax.all_to_all(partial.reshape(16, 8, 512), Q, 0, 0, tiled=True)  26.7 us
    all_to_all x1, waiting for transfers between devices, spread(): return lax.all_to_all(copies, axes, 0, 0, tiled=True)  21.7 us
    all_to_all x1, starting transfers between devices, spread(): return lax.all_to_all(copies, axes, 0, 0, tiled=True)  19.1 us
    ppermute x11, waiting for transfers between devices, move(): return lax.ppermute(value, AXES, pairs)  15.9 us
    all_gather x1, blocking collectives, on_device(): basis_rows = lax.all_gather(basis, 'c', axis=0, tiled=True)  8.9 us
    pallas_call x4, Pallas kernels, call(): pl.pallas_call(kernel, out_shape=jax.ShapeDtypeStruct((count, 896), f32),...  5 us
  transfers between devices with their start and end apart: 14, of which 6 were waited for; matrix products, arithmetic and copies ran while one was open for 3% of the time, Pallas kernels for 2%

profile of v2, /device:TPU:1, one launch (start us, length us, event | category | flops | bytes accessed | tf_op | source)
XLA Modules:
  0.0 201.8 jit_solution(3038091158326845703)
XLA Ops:
  9.6 8.9 %all_gather.7 = bf16[512,512]{1,0:T(8,128)(2,1)S(1)} all-gather(bf16[256,512]{1,0:T(8,128)(2,1)} %param.7), channel_id=1, replica_groups=mesh['zl'=4,'x'=4,'c'=2,'zh'=2,'y'=8] {'c'}, dimensions={0}, use_global_device_ids=true | all-gather | bytes 786432 | tf_op jit(solution)/shard_map/all_gather | solution.py:125
  19.5 26.7 %all-to-all-start = ((f32[16,8,512]{2,1,0:T(8,128)}), f32[16,8,512]{2,1,0:T(8,128)S(1)}, u32[]{:S(2)}, u32[]{:S(2)}) async-start(f32[16,8,512]{2,1,0:T(8,128)} %convolution_bitcast_fusion), calls=%async_computation | async-start | bytes 524288 | tf_op jit(solution)/shard_map/all_to_all | solution.py:128
  46.2 11.9 %collective-permute-start.1 = (bf16[128,512]{0,1:T(8,128)(2,1)S(1)}, bf16[128,512]{0,1:T(8,128)(2,1)S(1)}, u32[]{:S(2)}, u32[]{:S(2)}) collective-permute-start(bf16[128,512]{0,1:T(8,128)(2,1)S(1)} %collective-permute-done), channel_id=1, source_target_pairs={{0,8},{1,9},{2,10},{3,11},{4,12},{5,13},{6,14},{7,15},{8,0},{9,1},... | collective-permute-start | bytes 393224 | tf_op jit(solution)/shard_map/ppermute | solution.py:34
  58.1 5.9 %collective-permute-done.1 = bf16[128,512]{0,1:T(8,128)(2,1)S(1)} collective-permute-done((bf16[128,512]{0,1:T(8,128)(2,1)S(1)}, bf16[128,512]{0,1:T(8,128)(2,1)S(1)}, u32[]{:S(2)}, u32[]{:S(2)}) %collective-permute-start.1) | collective-permute-done | bytes 131104 | tf_op jit(solution)/shard_map/ppermute | solution.py:34
  64.9 19.1 %all-to-all-start.1 = ((f32[32,8,512]{2,1,0:T(8,128)}), f32[32,8,512]{2,1,0:T(8,128)S(1)}, u32[]{:S(2)}, u32[]{:S(2)}) async-start(f32[32,8,512]{2,1,0:T(8,128)} %broadcast_in_dim.8), calls=%async_computation.1 | async-start | bytes 1048576 | tf_op jit(solution)/shard_map/all_to_all | solution.py:56
  84.0 21.7 %all-to-all-done.1 = f32[32,8,512]{2,1,0:T(8,128)S(1)} async-done(((f32[32,8,512]{2,1,0:T(8,128)}), f32[32,8,512]{2,1,0:T(8,128)S(1)}, u32[]{:S(2)}, u32[]{:S(2)}) %all-to-all-start.1) | async-done | bytes 524320 | tf_op jit(solution)/shard_map/all_to_all | solution.py:56
  107.0 6.9 %collective-permute-start.3 = (f16[528,256]{1,0:T(8,128)(2,1)S(1)}, f16[528,256]{1,0:T(8,128)(2,1)S(1)}, u32[]{:S(2)}, u32[]{:S(2)}) collective-permute-start(f16[528,256]{1,0:T(8,128)(2,1)S(1)} %pad_maximum_fusion), channel_id=1, source_target_pairs={{0,7},{1,0},{2,1},{3,2},{4,3},{5,4},{6,5},{7,6},{8,15},{9,8},{10,9... | collective-permute-start | bytes 811016 | tf_op jit(solution)/shard_map/ppermute | solution.py:34
  113.9 1.9 collective-permute-start.2
  115.9 1.6 collective-permute-done.3
  117.5 5.3 %collective-permute-start.5 = (f16[528,256]{1,0:T(8,128)(2,1)S(1)}, f16[528,256]{1,0:T(8,128)(2,1)S(1)}, u32[]{:S(2)}, u32[]{:S(2)}) collective-permute-start(f16[528,256]{1,0:T(8,128)(2,1)S(1)} %collective-permute-done.3), channel_id=1, source_target_pairs={{0,7},{1,0},{2,1},{3,2},{4,3},{5,4},{6,5},{7,6},{8,15},{9,8},{10,9... | collective-permute-start | bytes 811016 | tf_op jit(solution)/shard_map/ppermute | solution.py:34
  122.8 1.9 collective-permute-start.4
  125.0 6.4 %collective-permute-done.4 = f16[528,256]{1,0:T(8,128)(2,1)} collective-permute-done((f16[528,256]{1,0:T(8,128)(2,1)S(1)}, f16[528,256]{1,0:T(8,128)(2,1)}, u32[]{:S(2)}, u32[]{:S(2)}) %collective-permute-start.4) | collective-permute-done | bytes 270368 | tf_op jit(solution)/shard_map/ppermute | solution.py:34
  131.4 1.9 collective-permute-start.6
  133.3 4.6 %collective-permute-start.7 = (f16[528,256]{1,0:T(8,128)(2,1)S(1)}, f16[528,256]{1,0:T(8,128)(2,1)S(1)}, u32[]{:S(2)}, u32[]{:S(2)}) collective-permute-start(f16[528,256]{1,0:T(8,128)(2,1)S(1)} %collective-permute-done.5), channel_id=1, source_target_pairs={{0,7},{1,0},{2,1},{3,2},{4,3},{5,4},{6,5},{7,6},{8,15},{9,8},{10,9... | collective-permute-start | bytes 811016 | tf_op jit(solution)/shard_map/ppermute | solution.py:34
  139.7 2.0 %copy-done = bf16[2048,896]{1,0:T(8,128)(2,1)S(1)} copy-done((bf16[2048,896]{1,0:T(8,128)(2,1)S(1)}, bf16[2048,896]{1,0:T(8,128)(2,1)}, u32[]{:S(2)}) %copy-start) | copy-done | bytes 3670040
  141.8 2.9 %shard_map.76.refs_4_ = f32[512,896]{1,0:T(8,128)S(1)} custom-call(s32[1]{0:T(128)} %bitcast.3.place, bf16[2,8,128,896]{3,2,1,0:T(8,128)(2,1)S(1)} %bitcast.47, bf16[512,256]{1,0:T(8,128)(2,1)S(1)} %reduce-precision_convert_fusion.6.refs_0_, bf16[512,256]{1,0:T(8,128)(2,1)S(1)} %get-tuple-element.20.refs_1_, bf16[512,256]{1,0:T(8,128)(2,1)S(1)} %get-tuple-element.35.refs_2_, ...), custom_call_target="tpu_custom_call" | custom-call | flops 2348810240 | bytes 10485760 | tf_op jit(solution)/shard_map/pallas_call | solution.py:104
  144.7 1.9 collective-permute-start.8
  146.7 4.6 %collective-permute-start.9 = (f16[528,128]{1,0:T(8,128)(2,1)S(1)}, f16[528,128]{1,0:T(8,128)(2,1)S(1)}, u32[]{:S(2)}, u32[]{:S(2)}) collective-permute-start(f16[528,128]{1,0:T(8,128)(2,1)S(1)} %slice.66), channel_id=1, source_target_pairs={{0,7},{1,0},{2,1},{3,2},{4,3},{5,4},{6,5},{7,6},{8,15},{9,8},{10,9... | collective-permute-start | bytes 405512 | tf_op jit(solution)/shard_map/ppermute | solution.py:34
  151.5 1.3 shard_map.77.total
  153.8 8.2 %collective-permute-start.10 = (f32[256,896]{1,0:T(8,128)S(1)}, f32[256,896]{1,0:T(8,128)S(1)}, u32[]{:S(2)}, u32[]{:S(2)}) collective-permute-start(f32[256,896]{1,0:T(8,128)S(1)} %shard_map.79), channel_id=1, source_target_pairs={{0,16},{1,17},{2,18},{3,19},{4,20},{5,21},{6,22},{7,23},{8,24},{9,... | collective-permute-start | bytes 2752520 | tf_op jit(solution)/shard_map/ppermute | solution.py:34
  162.5 1.6 collective-permute-done.10
  164.3 17.3 %all_to_all.20 = f32[64,1,128]{2,1,0:T(1,128)S(1)} all-to-all(f32[64,1,128]{2,1,0:T(1,128)S(1)} %broadcast_in_dim.10), channel_id=1, replica_groups=mesh['zl'=4,'x'=4,'c'=2,'zh'=2,'y'=8] {'x','c','y'}, dimensions={0} | all-to-all | bytes 65536 | tf_op jit(solution)/shard_map/all_to_all | solution.py:56
  181.6 10.4 %all_to_all.21 = f32[8,1,128]{2,1,0:T(1,128)S(1)} all-to-all(f32[8,1,128]{2,1,0:T(1,128)S(1)} %broadcast_in_dim.11), channel_id=1, replica_groups=mesh['zl'=4,'x'=4,'c'=2,'zh'=2,'y'=8] {'zh','zl'}, dimensions={0} | all-to-all | bytes 8192 | tf_op jit(solution)/shard_map/all_to_all | solution.py:56
  193.3 1.6 divide_convert_fusion
  (57 shorter events, 10.2 us)
Async XLA Ops:
  7.2 132.6 %all-gather.2.cloned.1.call-start = ((), (), s32[]{:S(2)}) async-start(), calls=%async_computation.4 | async-start | bytes 3899392 | tf_op jit(solution)/shard_map/all_gather | solution.py:120
  8.9 9.6 %collective-permute-start = (bf16[128,512]{0,1:T(8,128)(2,1)S(1)}, bf16[128,512]{0,1:T(8,128)(2,1)S(1)}, u32[]{:S(2)}, u32[]{:S(2)}) collective-permute-start(bf16[128,512]{0,1:T(8,128)(2,1)S(1)} %copy.16), channel_id=1, source_target_pairs={{0,0},{1,32},{2,64},{3,96},{4,128},{5,160},{6,192},{7,224},{8,256}... | collective-permute-start | bytes 393224 | tf_op jit(solution)/shard_map/ppermute | solution.py:34
  19.5 38.6 %all-to-all-start = ((f32[16,8,512]{2,1,0:T(8,128)}), f32[16,8,512]{2,1,0:T(8,128)S(1)}, u32[]{:S(2)}, u32[]{:S(2)}) async-start(f32[16,8,512]{2,1,0:T(8,128)} %convolution_bitcast_fusion), calls=%async_computation | async-start | bytes 524288 | tf_op jit(solution)/shard_map/all_to_all | solution.py:128
  46.2 17.9 %collective-permute-start.1 = (bf16[128,512]{0,1:T(8,128)(2,1)S(1)}, bf16[128,512]{0,1:T(8,128)(2,1)S(1)}, u32[]{:S(2)}, u32[]{:S(2)}) collective-permute-start(bf16[128,512]{0,1:T(8,128)(2,1)S(1)} %collective-permute-done), channel_id=1, source_target_pairs={{0,8},{1,9},{2,10},{3,11},{4,12},{5,13},{6,14},{7,15},{8,0},{9,1},... | collective-permute-start | bytes 393224 | tf_op jit(solution)/shard_map/ppermute | solution.py:34
  64.9 40.8 %all-to-all-start.1 = ((f32[32,8,512]{2,1,0:T(8,128)}), f32[32,8,512]{2,1,0:T(8,128)S(1)}, u32[]{:S(2)}, u32[]{:S(2)}) async-start(f32[32,8,512]{2,1,0:T(8,128)} %broadcast_in_dim.8), calls=%async_computation.1 | async-start | bytes 1048576 | tf_op jit(solution)/shard_map/all_to_all | solution.py:56
  107.0 10.5 %collective-permute-start.3 = (f16[528,256]{1,0:T(8,128)(2,1)S(1)}, f16[528,256]{1,0:T(8,128)(2,1)S(1)}, u32[]{:S(2)}, u32[]{:S(2)}) collective-permute-start(f16[528,256]{1,0:T(8,128)(2,1)S(1)} %pad_maximum_fusion), channel_id=1, source_target_pairs={{0,7},{1,0},{2,1},{3,2},{4,3},{5,4},{6,5},{7,6},{8,15},{9,8},{10,9... | collective-permute-start | bytes 811016 | tf_op jit(solution)/shard_map/ppermute | solution.py:34
  113.9 9.0 %collective-permute-start.2 = (f16[528,256]{1,0:T(8,128)(2,1)S(1)}, f16[528,256]{1,0:T(8,128)(2,1)S(1)}, u32[]{:S(2)}, u32[]{:S(2)}) collective-permute-start(f16[528,256]{1,0:T(8,128)(2,1)S(1)} %pad_maximum_fusion), channel_id=1, source_target_pairs={{0,1},{1,2},{2,3},{3,4},{4,5},{5,6},{6,7},{7,0},{8,9},{9,10},{10,1... | collective-permute-start | bytes 811016 | tf_op jit(solution)/shard_map/ppermute | solution.py:34
  117.5 15.8 %collective-permute-start.5 = (f16[528,256]{1,0:T(8,128)(2,1)S(1)}, f16[528,256]{1,0:T(8,128)(2,1)S(1)}, u32[]{:S(2)}, u32[]{:S(2)}) collective-permute-start(f16[528,256]{1,0:T(8,128)(2,1)S(1)} %collective-permute-done.3), channel_id=1, source_target_pairs={{0,7},{1,0},{2,1},{3,2},{4,3},{5,4},{6,5},{7,6},{8,15},{9,8},{10,9... | collective-permute-start | bytes 811016 | tf_op jit(solution)/shard_map/ppermute | solution.py:34
  122.8 8.5 %collective-permute-start.4 = (f16[528,256]{1,0:T(8,128)(2,1)S(1)}, f16[528,256]{1,0:T(8,128)(2,1)}, u32[]{:S(2)}, u32[]{:S(2)}) collective-permute-start(f16[528,256]{1,0:T(8,128)(2,1)S(1)} %collective-permute-done.2), channel_id=1, source_target_pairs={{0,1},{1,2},{2,3},{3,4},{4,5},{5,6},{6,7},{7,0},{8,9},{9,10},{10,1... | collective-permute-start | bytes 811016 | tf_op jit(solution)/shard_map/ppermute | solution.py:34
  131.4 13.3 %collective-permute-start.6 = (f16[528,256]{1,0:T(8,128)(2,1)}, f16[528,256]{1,0:T(8,128)(2,1)S(1)}, u32[]{:S(2)}, u32[]{:S(2)}) collective-permute-start(f16[528,256]{1,0:T(8,128)(2,1)} %collective-permute-done.4), channel_id=1, source_target_pairs={{0,1},{1,2},{2,3},{3,4},{4,5},{5,6},{6,7},{7,0},{8,9},{9,10},{10,1... | collective-permute-start | bytes 811016 | tf_op jit(solution)/shard_map/ppermute | solution.py:34
  133.3 11.4 %collective-permute-start.7 = (f16[528,256]{1,0:T(8,128)(2,1)S(1)}, f16[528,256]{1,0:T(8,128)(2,1)S(1)}, u32[]{:S(2)}, u32[]{:S(2)}) collective-permute-start(f16[528,256]{1,0:T(8,128)(2,1)S(1)} %collective-permute-done.5), channel_id=1, source_target_pairs={{0,7},{1,0},{2,1},{3,2},{4,3},{5,4},{6,5},{7,6},{8,15},{9,8},{10,9... | collective-permute-start | bytes 811016 | tf_op jit(solution)/shard_map/ppermute | solution.py:34
  139.7 2.0 %copy-start = (bf16[2048,896]{1,0:T(8,128)(2,1)S(1)}, bf16[2048,896]{1,0:T(8,128)(2,1)}, u32[]{:S(2)}) copy-start(bf16[2048,896]{1,0:T(8,128)(2,1)} %all-gather.2.cloned.1.call-done) | copy-start | bytes 11010052
  144.7 8.0 %collective-permute-start.8 = (f16[528,128]{1,0:T(8,128)(2,1)S(1)}, f16[528,128]{1,0:T(8,128)(2,1)S(1)}, u32[]{:S(2)}, u32[]{:S(2)}) collective-permute-start(f16[528,128]{1,0:T(8,128)(2,1)S(1)} %slice.63), channel_id=1, source_target_pairs={{0,1},{1,2},{2,3},{3,4},{4,5},{5,6},{6,7},{7,0},{8,9},{9,10},{10,1... | collective-permute-start | bytes 405512 | tf_op jit(solution)/shard_map/ppermute | solution.py:34
  146.7 6.5 %collective-permute-start.9 = (f16[528,128]{1,0:T(8,128)(2,1)S(1)}, f16[528,128]{1,0:T(8,128)(2,1)S(1)}, u32[]{:S(2)}, u32[]{:S(2)}) collective-permute-start(f16[528,128]{1,0:T(8,128)(2,1)S(1)} %slice.66), channel_id=1, source_target_pairs={{0,7},{1,0},{2,1},{3,2},{4,3},{5,4},{6,5},{7,6},{8,15},{9,8},{10,9... | collective-permute-start | bytes 405512 | tf_op jit(solution)/shard_map/ppermute | solution.py:34
  153.8 39.5 %copy-start.1 = (f32[256,896]{1,0:T(8,128)S(1)}, f32[256,896]{1,0:T(8,128)}, u32[]{:S(2)}) copy-start(f32[256,896]{1,0:T(8,128)} %param.9) | copy-start | bytes 2752516
  153.8 39.5 %copy-start.2 = (f32[256,896]{1,0:T(8,128)S(1)}, f32[256,896]{1,0:T(8,128)}, u32[]{:S(2)}) copy-start(f32[256,896]{1,0:T(8,128)} %param.8) | copy-start | bytes 2752516
  153.8 10.3 %collective-permute-start.10 = (f32[256,896]{1,0:T(8,128)S(1)}, f32[256,896]{1,0:T(8,128)S(1)}, u32[]{:S(2)}, u32[]{:S(2)}) collective-permute-start(f32[256,896]{1,0:T(8,128)S(1)} %shard_map.79), channel_id=1, source_target_pairs={{0,16},{1,17},{2,18},{3,19},{4,20},{5,21},{6,22},{7,23},{8,24},{9,... | collective-permute-start | bytes 2752520 | tf_op jit(solution)/shard_map/ppermute | solution.py:34
Sparse Core Ops, SparseCore 0:
  10.1 102.1 all-gather.1

commit v3 on v2

v3 whole, which is shorter than its diff:
```python
import jax
import jax.numpy as jnp
from jax import lax
from jax.experimental import pallas as pl
from jax.experimental.pallas import tpu as pltpu
from jax.sharding import Mesh, PartitionSpec as P

D = 8192
FF = 14336
ZL, X, C, ZH, Y = 4, 4, 2, 2, 8
AXES = ("zl", "x", "c", "zh", "y")
DP = ("zl", "x", "c")
MP = ("zh", "y")
Q = ("zl", "x")
f32 = jnp.float32
bf16 = jnp.bfloat16
f16 = jnp.float16


def move(value, to):
    def index(zl, x, c, zh, y):
        return (((zl * X + x) * C + c) * ZH + zh) * Y + y

    pairs = [
        (index(zl, x, c, zh, y), index(*to(zl, x, c, zh, y)))
        for zl in range(ZL)
        for x in range(X)
        for c in range(C)
        for zh in range(ZH)
        for y in range(Y)
    ]
    return lax.ppermute(value, AXES, pairs)


def transpose_place(zl, x, c, zh, y):
    j = Y * zh + y
    return j // X, j % X, c, zl // 2, 2 * x + zl % 2


def other_core(value):
    return move(value, lambda zl, x, c, zh, y: (zl, x, 1 - c, zh, y))


def other_half(value):
    return move(value, lambda zl, x, c, zh, y: (zl, x, c, 1 - zh, y))


def spread(value, axes, n):
    copies = jnp.broadcast_to(value[None], (n,) + value.shape)
    return lax.all_to_all(copies, axes, 0, 0, tiled=True)


def parts(value, n):
    out = []
    for _ in range(n - 1):
        top = lax.reduce_precision(value, 8, 7)
        out.append(top.astype(bf16))
        value = value - top
    return out + [value.astype(bf16)]


def code(value):
    largest = jnp.max(jnp.abs(value), axis=0, keepdims=True)
    scale = lax.reduce_precision(jnp.maximum(largest * 2.0**-6, 2.0**-14), 5, 10)
    scale = jnp.where(scale * 2.0**6 < largest, scale * (1 + 2.0**-9), scale)
    scale = lax.reduce_precision(scale, 5, 10)
    share = value / (scale * 2.0**6)
    size = jnp.exp2(29.0 * jnp.abs(share) - 14.0)
    coded = jnp.where(share < 0, -size, size).astype(f16)
    return jnp.concatenate([coded, jnp.broadcast_to(scale, (16, 512)).astype(f16)])


def decode(blocks):
    coded = blocks[:, :256].astype(f32)
    share = (jnp.log2(jnp.abs(coded)) + 14.0) / 29.0
    share = jnp.where(coded < 0, -share, share)
    return parts(share * (blocks[:, 256:257].astype(f32) * 2.0**6), 2)


def grad_kernel(core, g_ref, high, low, out):
    rows = pl.ds(pl.multiple_of(core[0] * 256, 256), 256)
    value = None
    for y in range(Y):
        tokens = [g_ref[(2 * zh + y % 2) * X + y // 2] for zh in range(ZH)]
        tokens = jnp.concatenate(tokens, axis=0)
        for block in (high, low):
            term = lax.dot_general(
                block[y, :, rows],
                tokens,
                (((0,), (0,)), ((), ())),
                preferred_element_type=f32,
            )
            value = term if value is None else value + term
    out[...] = value


def call(kernel, core, g, given):
    vmem = pl.BlockSpec(memory_space=pltpu.VMEM)
    return pl.pallas_call(
        kernel,
        out_shape=jax.ShapeDtypeStruct((256, 896), f32),
        in_specs=[pl.BlockSpec(memory_space=pltpu.SMEM), vmem] + [vmem] * len(given),
        out_specs=vmem,
        compiler_params=pltpu.CompilerParams(vmem_limit_bytes=16 * 2**20),
        cost_estimate=pl.CostEstimate(
            flops=4 * 2048 * 256 * 896, bytes_accessed=8 * 2**20, transcendentals=0
        ),
    )(core.astype(jnp.int32).reshape(1), g, *given)


def on_device(features, output_grads, basis, moment_one, moment_two):
    c, zh, y = lax.axis_index("c"), lax.axis_index("zh"), lax.axis_index("y")
    g = lax.all_gather(output_grads, Q, axis=0)

    own = move(features, transpose_place)
    far = other_half(own)
    basis_rows = lax.all_gather(basis, "c", axis=0, tiled=True)

    partial = jnp.dot(own, basis_rows, preferred_element_type=f32)
    pieces = lax.all_to_all(partial.reshape(16, 8, 512), Q, 0, 0, tiled=True)
    summed, own, far = lax.optimization_barrier((jnp.sum(pieces, axis=0), own, far))
    both = jnp.concatenate([jnp.where(zh == 0, own, far), jnp.where(zh == 0, far, own)])
    coded = spread(summed, ("zh",) + Q, 32).reshape(256, 512)
    away = sum(
        lax.dot_general(
            p, basis_rows, (((1,), (1,)), ((), ())), preferred_element_type=f32
        )
        for p in parts(coded, 3)
    )
    kept = code(both.astype(f32) - away)

    blocks = lax.all_gather(kept, "y", axis=0)

    high, low = decode(blocks)

    def products(core):
        return call(grad_kernel, core, g, [high, low])

    received = other_core(products(1 - c))
    projected = products(c) + received

    squares = jnp.sum((projected * projected).reshape(256, 7, 128), axis=(0, 1))
    squares = jnp.sum(spread(squares[None], ("x", "c", "y"), 64), axis=0)
    square_sum = jnp.sum(spread(squares, ("zh", "zl"), 8))
    mean_square = square_sum / (D * FF)
    factor = jnp.minimum(1.0, lax.rsqrt(mean_square + 1e-06))
    clipped = factor * projected
    new_one = 0.9 * moment_one + 0.1 * clipped
    new_two = 0.95 * moment_two + 0.05 * clipped * clipped
    update = (new_one / (jnp.sqrt(new_two) + 1e-08)).astype(bf16)
    return (new_one, new_two, update)


def solution(mesh):
    fine = Mesh(mesh.devices.reshape(ZL, X, C, ZH, Y), AXES)
    tile = P(DP, MP)
    return jax.shard_map(
        on_device,
        mesh=fine,
        in_specs=(tile, tile, P(DP, None), tile, tile),
        out_specs=(tile, tile, tile),
        check_vma=False,
    )
```

time: 203 us -> 191 us (0.941)
  starting transfers between devices: 95.6 us -> 65.2 us
  blocking collectives: 36.5 us -> 62.4 us
  waiting for transfers between devices: 38.4 us -> 29.6 us
  other arithmetic: 5.16 us -> 7.31 us
    ppermute x11 -> x3, starting transfers between devices: 49.8 us -> 21.3 us  [move(): return lax.ppermute(value, AXES, pairs)]
    all_gather x0 -> x1, blocking collectives: none -> 28.2 us  [on_device(): blocks = lax.all_gather(kept, 'y', axis=0)]
    ppermute x11 -> x3, waiting for transfers between devices: 15.9 us -> 7.29 us  [move(): return lax.ppermute(value, AXES, pairs)]
    all_to_all x2, blocking collectives: 27.6 us -> 25.3 us  [spread(): return lax.all_to_all(copies, axes, 0, 0, tiled=True)]
    pallas_call x4 -> x2, Pallas kernels: 5 us -> 4.76 us  [call(): pl.pallas_call(kernel, out_shape=jax.ShapeDtypeStruct((256, 896), f32), i...]
  transfers between devices with their start and end apart: 14 -> 6, of which waited for: 6 -> 2; matrix products, arithmetic and copies ran while one was open for 3% -> 3% of each run, Pallas kernels for 2% -> 1%
where the time goes in v3:
time: 191 us
  starting transfers between devices  65.2 us (34%)
  blocking collectives  62.4 us (33%)
  waiting for transfers between devices  29.6 us (15%)
  between operations  14.9 us (8%)
  other arithmetic  7.31 us (4%)
  Pallas kernels  4.76 us (2%)
  local copies, waits for them, and re-layouts  4.54 us (2%)
  matrix products  1.96 us (1%)
    all_gather x1, blocking collectives, on_device(): blocks = lax.all_gather(kept, 'y', axis=0)  28.2 us
    all_to_all x1, starting transfers between devices, on_device(): pieces = lax.all_to_all(partial.reshape(16, 8, 512), Q, 0, 0, tiled=True)  26.2 us
    all_to_all x2, blocking collectives, spread(): return lax.all_to_all(copies, axes, 0, 0, tiled=True)  25.3 us
    all_to_all x1, waiting for transfers between devices, spread(): return lax.all_to_all(copies, axes, 0, 0, tiled=True)  21.6 us
    ppermute x3, starting transfers between devices, move(): return lax.ppermute(value, AXES, pairs)  21.3 us
    all_to_all x1, starting transfers between devices, spread(): return lax.all_to_all(copies, axes, 0, 0, tiled=True)  17.7 us
    all_gather x1, blocking collectives, on_device(): basis_rows = lax.all_gather(basis, 'c', axis=0, tiled=True)  8.89 us
    ppermute x3, waiting for transfers between devices, move(): return lax.ppermute(value, AXES, pairs)  7.29 us
  transfers between devices with their start and end apart: 6, of which 2 were waited for; matrix products, arithmetic and copies ran while one was open for 3% of the time, Pallas kernels for 1%

profile of v3, /device:TPU:1, one launch (start us, length us, event | category | flops | bytes accessed | tf_op | source)
XLA Modules:
  0.0 190.7 jit_solution(5010597347550153718)
XLA Ops:
  7.2 0.7 all-gather.5.cloned.1.call-update
  7.9 1.6 collective-permute-start
  9.5 8.9 %all_gather.17 = bf16[512,512]{1,0:T(8,128)(2,1)S(1)} all-gather(bf16[256,512]{1,0:T(8,128)(2,1)} %param.7), channel_id=1, replica_groups=mesh['zl'=4,'x'=4,'c'=2,'zh'=2,'y'=8] {'c'}, dimensions={0}, use_global_device_ids=true | all-gather | bytes 786432 | tf_op jit(solution)/shard_map/all_gather | solution.py:117
  18.3 0.9 convolution_bitcast_fusion
  19.3 26.2 %all-to-all-start = ((f32[16,8,512]{2,1,0:T(8,128)}), f32[16,8,512]{2,1,0:T(8,128)S(1)}, u32[]{:S(2)}, u32[]{:S(2)}) async-start(f32[16,8,512]{2,1,0:T(8,128)} %convolution_bitcast_fusion), calls=%async_computation | async-start | bytes 524288 | tf_op jit(solution)/shard_map/all_to_all | solution.py:120
  45.5 11.5 %collective-permute-start.1 = (bf16[128,512]{1,0:T(8,128)(2,1)S(1)}, bf16[128,512]{1,0:T(8,128)(2,1)S(1)}, u32[]{:S(2)}, u32[]{:S(2)}) collective-permute-start(bf16[128,512]{1,0:T(8,128)(2,1)S(1)} %collective-permute-done), channel_id=1, source_target_pairs={{0,8},{1,9},{2,10},{3,11},{4,12},{5,13},{6,14},{7,15},{8,0},{9,1},... | collective-permute-start | bytes 393224 | tf_op jit(solution)/shard_map/ppermute | solution.py:32
  57.0 7.3 %collective-permute-done.1 = bf16[128,512]{1,0:T(8,128)(2,1)S(1)} collective-permute-done((bf16[128,512]{1,0:T(8,128)(2,1)S(1)}, bf16[128,512]{1,0:T(8,128)(2,1)S(1)}, u32[]{:S(2)}, u32[]{:S(2)}) %collective-permute-start.1) | collective-permute-done | bytes 131104 | tf_op jit(solution)/shard_map/ppermute | solution.py:32
  64.3 0.9 broadcast_in_dim.8
  65.2 17.7 %all-to-all-start.1 = ((f32[32,8,512]{2,1,0:T(8,128)}), f32[32,8,512]{2,1,0:T(8,128)S(1)}, u32[]{:S(2)}, u32[]{:S(2)}) async-start(f32[32,8,512]{2,1,0:T(8,128)} %broadcast_in_dim.8), calls=%async_computation.1 | async-start | bytes 1048576 | tf_op jit(solution)/shard_map/all_to_all | solution.py:50
  82.9 21.6 %all-to-all-done.1 = f32[32,8,512]{2,1,0:T(8,128)S(1)} async-done(((f32[32,8,512]{2,1,0:T(8,128)}), f32[32,8,512]{2,1,0:T(8,128)S(1)}, u32[]{:S(2)}, u32[]{:S(2)}) %all-to-all-start.1) | async-done | bytes 524320 | tf_op jit(solution)/shard_map/all_to_all | solution.py:50
  104.6 0.3 fusion.11
  104.9 0.3 convolution_add_fusion.1
  105.3 0.4 abs_reduce_fusion
  106.0 28.2 %all-gather.6 = f16[2176,512]{1,0:T(8,128)(2,1)S(1)} all-gather(f16[272,512]{1,0:T(8,128)(2,1)S(1)} %pad_maximum_fusion), channel_id=3, replica_groups=mesh['zl'=4,'x'=4,'c'=2,'zh'=2,'y'=8] {'y'}, dimensions={0}, use_global_device_ids=true | all-gather | bytes 2506752 | tf_op jit(solution)/shard_map/all_gather | solution.py:132
  134.2 3.3 %fusion.4 = (bf16[8,256,512]{2,1,0:T(8,128)(2,1)S(1)}, bf16[8,256,512]{2,1,0:T(8,128)(2,1)}) fusion(f32[8,512]{1,0:T(8,128)S(1)} %bitcast.35, f16[8,272,512]{2,1,0:T(8,128)(2,1)S(1)} %bitcast.33), kind=kLoop, calls=%fused_computation.9 | loop fusion | flops 13631488 | bytes 6307840 | tf_op jit(solution)/shard_map/convert_element_type | solution.py:59
  137.5 1.6 copy-done
  139.1 2.0 %copy-done.2 = bf16[2048,896]{1,0:T(8,128)(2,1)S(1)} copy-done((bf16[2048,896]{1,0:T(8,128)(2,1)S(1)}, bf16[2048,896]{1,0:T(8,128)(2,1)}, u32[]{:S(2)}) %copy-start.2) | copy-done | bytes 3670040
  141.2 2.4 %shard_map.77 = f32[256,896]{1,0:T(8,128)S(1)} custom-call(s32[1]{0:T(128)} %bitcast.5.core, bf16[16,128,896]{2,1,0:T(8,128)(2,1)S(1)} %bitcast.30, bf16[8,256,512]{2,1,0:T(8,128)(2,1)S(1)} %copy-done, bf16[8,256,512]{2,1,0:T(8,128)(2,1)S(1)} %get-tuple-element.14.low), custom_call_target="tpu_custom_call" | custom-call | flops 1879048192 | bytes 8388608 | tf_op jit(solution)/shard_map/pallas_call | solution.py:99
  143.5 8.2 %collective-permute-start.2 = (f32[256,896]{1,0:T(8,128)S(1)}, f32[256,896]{1,0:T(8,128)S(1)}, u32[]{:S(2)}, u32[]{:S(2)}) collective-permute-start(f32[256,896]{1,0:T(8,128)S(1)} %shard_map.77), channel_id=1, source_target_pairs={{0,16},{1,17},{2,18},{3,19},{4,20},{5,21},{6,22},{7,23},{8,24},{9,... | collective-permute-start | bytes 2752520 | tf_op jit(solution)/shard_map/ppermute | solution.py:32
  151.8 2.4 %shard_map.76 = f32[256,896]{1,0:T(8,128)S(1)} custom-call(s32[1]{0:T(128)} %bitcast.core, bf16[16,128,896]{2,1,0:T(8,128)(2,1)S(1)} %bitcast.31, bf16[8,256,512]{2,1,0:T(8,128)(2,1)S(1)} %copy-done.1, bf16[8,256,512]{2,1,0:T(8,128)(2,1)S(1)} %get-tuple-element.14.low), custom_call_target="tpu_custom_call" | custom-call | flops 1879048192 | bytes 8388608 | tf_op jit(solution)/shard_map/pallas_call | solution.py:99
  154.4 15.6 %all_to_all.20 = f32[64,1,128]{2,1,0:T(1,128)S(1)} all-to-all(f32[64,1,128]{2,1,0:T(1,128)S(1)} %broadcast_in_dim.10), channel_id=1, replica_groups=mesh['zl'=4,'x'=4,'c'=2,'zh'=2,'y'=8] {'x','c','y'}, dimensions={0} | all-to-all | bytes 65536 | tf_op jit(solution)/shard_map/all_to_all | solution.py:50
  170.0 9.7 %all_to_all.21 = f32[8,1,128]{2,1,0:T(1,128)S(1)} all-to-all(f32[8,1,128]{2,1,0:T(1,128)S(1)} %broadcast_in_dim.11), channel_id=1, replica_groups=mesh['zl'=4,'x'=4,'c'=2,'zh'=2,'y'=8] {'zh','zl'}, dimensions={0} | all-to-all | bytes 8192 | tf_op jit(solution)/shard_map/all_to_all | solution.py:50
  179.7 0.6 reduce_sum.48
  181.0 2.8 %divide_convert_fusion = (bf16[256,896]{1,0:T(8,128)(2,1)}, f32[256,896]{1,0:T(8,128)}, f32[256,896]{1,0:T(8,128)}) fusion(f32[256,896]{1,0:T(8,128)S(1)} %get-tuple-element.13, f32[]{:T(128)S(6)} %min_shard_map.3, f32[256,896]{1,0:T(8,128)S(1)} %copy-done.4, f32[256,896]{1,0:T(8,128)} %param.8), kind=kLoop, calls=%fused_computation.17 | loop fusion | flops 2523136 | bytes 5046276 | tf_op jit(solution)/shard_map/convert_element_type | solution.py:150
  (26 shorter events, 0.6 us)
Async XLA Ops:
  7.2 130.4 %all-gather.5.cloned.1.call-start = ((), (), s32[]{:S(2)}) async-start(), calls=%async_computation.4 | async-start | bytes 3899392 | tf_op jit(solution)/shard_map/all_gather | solution.py:113
  7.9 10.5 %collective-permute-start = (bf16[128,512]{1,0:T(8,128)(2,1)}, bf16[128,512]{1,0:T(8,128)(2,1)S(1)}, u32[]{:S(2)}, u32[]{:S(2)}) collective-permute-start(bf16[128,512]{1,0:T(8,128)(2,1)} %param.5), channel_id=1, source_target_pairs={{0,0},{1,32},{2,64},{3,96},{4,128},{5,160},{6,192},{7,224},{8,256}... | collective-permute-start | bytes 393224 | tf_op jit(solution)/shard_map/ppermute | solution.py:32
  19.3 37.7 %all-to-all-start = ((f32[16,8,512]{2,1,0:T(8,128)}), f32[16,8,512]{2,1,0:T(8,128)S(1)}, u32[]{:S(2)}, u32[]{:S(2)}) async-start(f32[16,8,512]{2,1,0:T(8,128)} %convolution_bitcast_fusion), calls=%async_computation | async-start | bytes 524288 | tf_op jit(solution)/shard_map/all_to_all | solution.py:120
  45.5 18.8 %collective-permute-start.1 = (bf16[128,512]{1,0:T(8,128)(2,1)S(1)}, bf16[128,512]{1,0:T(8,128)(2,1)S(1)}, u32[]{:S(2)}, u32[]{:S(2)}) collective-permute-start(bf16[128,512]{1,0:T(8,128)(2,1)S(1)} %collective-permute-done), channel_id=1, source_target_pairs={{0,8},{1,9},{2,10},{3,11},{4,12},{5,13},{6,14},{7,15},{8,0},{9,1},... | collective-permute-start | bytes 393224 | tf_op jit(solution)/shard_map/ppermute | solution.py:32
  65.2 39.4 %all-to-all-start.1 = ((f32[32,8,512]{2,1,0:T(8,128)}), f32[32,8,512]{2,1,0:T(8,128)S(1)}, u32[]{:S(2)}, u32[]{:S(2)}) async-start(f32[32,8,512]{2,1,0:T(8,128)} %broadcast_in_dim.8), calls=%async_computation.1 | async-start | bytes 1048576 | tf_op jit(solution)/shard_map/all_to_all | solution.py:50
  137.5 1.6 copy-start
  139.1 2.0 %copy-start.2 = (bf16[2048,896]{1,0:T(8,128)(2,1)S(1)}, bf16[2048,896]{1,0:T(8,128)(2,1)}, u32[]{:S(2)}) copy-start(bf16[2048,896]{1,0:T(8,128)(2,1)} %all-gather.5.cloned.1.call-done) | copy-start | bytes 11010052
  141.1 10.6 %copy-start.1 = (bf16[8,256,512]{2,1,0:T(8,128)(2,1)S(1)}, bf16[8,256,512]{2,1,0:T(8,128)(2,1)}, u32[]{:S(2)}) copy-start(bf16[8,256,512]{2,1,0:T(8,128)(2,1)} %get-tuple-element.15.high) | copy-start | bytes 6291460
  141.1 10.6 %copy-start.3 = (bf16[2048,896]{1,0:T(8,128)(2,1)S(1)}, bf16[2048,896]{1,0:T(8,128)(2,1)}, u32[]{:S(2)}) copy-start(bf16[2048,896]{1,0:T(8,128)(2,1)} %all-gather.5.cloned.1.call-done) | copy-start | bytes 11010052
  143.5 10.6 %collective-permute-start.2 = (f32[256,896]{1,0:T(8,128)S(1)}, f32[256,896]{1,0:T(8,128)S(1)}, u32[]{:S(2)}, u32[]{:S(2)}) collective-permute-start(f32[256,896]{1,0:T(8,128)S(1)} %shard_map.77), channel_id=1, source_target_pairs={{0,16},{1,17},{2,18},{3,19},{4,20},{5,21},{6,22},{7,23},{8,24},{9,... | collective-permute-start | bytes 2752520 | tf_op jit(solution)/shard_map/ppermute | solution.py:32
  151.8 29.2 %copy-start.4 = (f32[256,896]{1,0:T(8,128)S(1)}, f32[256,896]{1,0:T(8,128)}, u32[]{:S(2)}) copy-start(f32[256,896]{1,0:T(8,128)} %param.9) | copy-start | bytes 2752516
Sparse Core Ops, SparseCore 0:
  10.1 100.5 all-gather.4

commit v4 on v3

--- a/solution.py
+++ b/solution.py
@@ -72,16 +72,16 @@
 
 def decode(blocks):
     coded = blocks[:, :256].astype(f32)
-    share = (jnp.log2(jnp.abs(coded)) + 14.0) / 29.0
-    share = jnp.where(coded < 0, -share, share)
-    return parts(share * (blocks[:, 256:257].astype(f32) * 2.0**6), 2)
+    scale = blocks[:, 256:257].astype(f32) * (2.0**6 / 29.0)
+    size = jnp.log2(jnp.abs(coded)) * scale + 14.0 * scale
+    return parts(jnp.where(coded < 0, -size, size), 2)
 
 
 def grad_kernel(core, g_ref, high, low, out):
     rows = pl.ds(pl.multiple_of(core[0] * 256, 256), 256)
     value = None
     for y in range(Y):
-        tokens = [g_ref[(2 * zh + y % 2) * X + y // 2] for zh in range(ZH)]
+        tokens = [g_ref[y // 2, 2 * zh + y % 2] for zh in range(ZH)]
         tokens = jnp.concatenate(tokens, axis=0)
         for block in (high, low):
             term = lax.dot_general(
@@ -101,7 +101,7 @@
         out_shape=jax.ShapeDtypeStruct((256, 896), f32),
         in_specs=[pl.BlockSpec(memory_space=pltpu.SMEM), vmem] + [vmem] * len(given),
         out_specs=vmem,
-        compiler_params=pltpu.CompilerParams(vmem_limit_bytes=16 * 2**20),
+        compiler_params=pltpu.CompilerParams(vmem_limit_bytes=8 * 2**20),
         cost_estimate=pl.CostEstimate(
             flops=4 * 2048 * 256 * 896, bytes_accessed=8 * 2**20, transcendentals=0
         ),
@@ -110,12 +110,14 @@
 
 def on_device(features, output_grads, basis, moment_one, moment_two):
     c, zh, y = lax.axis_index("c"), lax.axis_index("zh"), lax.axis_index("y")
-    g = lax.all_gather(output_grads, Q, axis=0)
-
     own = move(features, transpose_place)
-    far = other_half(own)
     basis_rows = lax.all_gather(basis, "c", axis=0, tiled=True)
 
+    shard, basis_rows = lax.optimization_barrier((output_grads, basis_rows))
+    column = lax.all_gather(shard, "zl", axis=0)
+    column, own = lax.optimization_barrier((column, own))
+    g = lax.all_gather(column, "x", axis=0)
+    far = other_half(own)
     partial = jnp.dot(own, basis_rows, preferred_element_type=f32)
     pieces = lax.all_to_all(partial.reshape(16, 8, 512), Q, 0, 0, tiled=True)
     summed, own, far = lax.optimization_barrier((jnp.sum(pieces, axis=0), own, far))
@@ -130,6 +132,7 @@
     kept = code(both.astype(f32) - away)
 
     blocks = lax.all_gather(kept, "y", axis=0)
+    blocks, g = lax.optimization_barrier((blocks, g))
 
     high, low = decode(blocks)
 

time: 191 us -> 181 us (0.948)
  blocking collectives: 62.4 us -> 106 us
  starting transfers between devices: 65.2 us -> 26.8 us
  waiting for transfers between devices: 29.6 us -> 20.5 us
  local copies, waits for them, and re-layouts: 4.54 us -> 1.16 us
  other arithmetic: 7.31 us -> 4.52 us
    all_gather x0 -> x1, blocking collectives: none -> 39.9 us  [on_device(): column = lax.all_gather(shard, 'zl', axis=0)]
    all_to_all x1, starting transfers between devices: 26.2 us -> 3.53 us  [on_device(): pieces = lax.all_to_all(partial.reshape(16, 8, 512), Q, 0, 0, tiled=True)]
    all_to_all x1, waiting for transfers between devices: 21.6 us -> 12.7 us  [spread(): return lax.all_to_all(copies, axes, 0, 0, tiled=True)]
    all_to_all x1, starting transfers between devices: 17.7 us -> 9.13 us  [spread(): return lax.all_to_all(copies, axes, 0, 0, tiled=True)]
    ppermute x3, starting transfers between devices: 21.3 us -> 14.1 us  [move(): return lax.ppermute(value, AXES, pairs)]
    all_to_all x1, waiting for transfers between devices: 0.01 us -> 6.97 us  [on_device(): pieces = lax.all_to_all(partial.reshape(16, 8, 512), Q, 0, 0, tiled=True)]
    ppermute x3, waiting for transfers between devices: 7.29 us -> 0.81 us  [move(): return lax.ppermute(value, AXES, pairs)]
    all_gather x1, blocking collectives: 28.2 us -> 31.9 us  [on_device(): blocks = lax.all_gather(kept, 'y', axis=0)]
  transfers between devices with their start and end apart: 6 -> 6, of which waited for: 2 -> 3; matrix products, arithmetic and copies ran while one was open for 3% -> 2% of each run, Pallas kernels for 1% -> 1%
where the time goes in v4:
time: 181 us
  blocking collectives  106 us (59%)
  starting transfers between devices  26.8 us (15%)
  waiting for transfers between devices  20.5 us (11%)
  between operations  14.9 us (8%)
  Pallas kernels  4.76 us (3%)
  other arithmetic  4.52 us (2%)
  matrix products  1.96 us (1%)
    all_gather x1, blocking collectives, on_device(): column = lax.all_gather(shard, 'zl', axis=0)  39.9 us
    all_gather x1, blocking collectives, on_device(): blocks = lax.all_gather(kept, 'y', axis=0)  31.9 us
    all_to_all x2, blocking collectives, spread(): return lax.all_to_all(copies, axes, 0, 0, tiled=True)  25.5 us
    ppermute x3, starting transfers between devices, move(): return lax.ppermute(value, AXES, pairs)  14.1 us
    all_to_all x1, waiting for transfers between devices, spread(): return lax.all_to_all(copies, axes, 0, 0, tiled=True)  12.7 us
    all_to_all x1, starting transfers between devices, spread(): return lax.all_to_all(copies, axes, 0, 0, tiled=True)  9.13 us
    all_gather x1, blocking collectives, on_device(): basis_rows = lax.all_gather(basis, 'c', axis=0, tiled=True)  8.89 us
    all_to_all x1, waiting for transfers between devices, on_device(): pieces = lax.all_to_all(partial.reshape(16, 8, 512), Q, 0, 0, tiled=True)  6.97 us
  transfers between devices with their start and end apart: 6, of which 3 were waited for; matrix products, arithmetic and copies ran while one was open for 2% of the time, Pallas kernels for 1%

profile of v4, /device:TPU:1, one launch (start us, length us, event | category | flops | bytes accessed | tf_op | source)
XLA Modules:
  0.0 180.7 jit_solution(17847155447012418057)
XLA Ops:
  7.2 1.6 collective-permute-start
  8.8 8.9 %all_gather.21 = bf16[512,512]{1,0:T(8,128)(2,1)S(1)} all-gather(bf16[256,512]{1,0:T(8,128)(2,1)} %param.7), channel_id=1, replica_groups=mesh['zl'=4,'x'=4,'c'=2,'zh'=2,'y'=8] {'c'}, dimensions={0}, use_global_device_ids=true | all-gather | bytes 786432 | tf_op jit(solution)/shard_map/all_gather | solution.py:114
  17.7 39.9 %all-gather = bf16[512,896]{1,0:T(8,128)(2,1)} all-gather(bf16[128,896]{1,0:T(8,128)(2,1)} %param.6), channel_id=2, replica_groups=mesh['zl'=4,'x'=4,'c'=2,'zh'=2,'y'=8] {'zl'}, dimensions={0}, use_global_device_ids=true | all-gather | bytes 1146880 | tf_op jit(solution)/shard_map/all_gather | solution.py:117
  57.5 0.9 convolution_bitcast_fusion
  58.5 3.5 %all-to-all-start = ((f32[16,8,512]{2,1,0:T(8,128)}), f32[16,8,512]{2,1,0:T(8,128)S(1)}, u32[]{:S(2)}, u32[]{:S(2)}) async-start(f32[16,8,512]{2,1,0:T(8,128)} %convolution_bitcast_fusion), calls=%async_computation | async-start | bytes 524288 | tf_op jit(solution)/shard_map/all_to_all | solution.py:122
  62.0 1.9 %collective-permute-start.1 = (bf16[128,512]{1,0:T(8,128)(2,1)S(1)}, bf16[128,512]{1,0:T(8,128)(2,1)S(1)}, u32[]{:S(2)}, u32[]{:S(2)}) collective-permute-start(bf16[128,512]{1,0:T(8,128)(2,1)S(1)} %collective-permute-done), channel_id=1, source_target_pairs={{0,8},{1,9},{2,10},{3,11},{4,12},{5,13},{6,14},{7,15},{8,0},{9,1},... | collective-permute-start | bytes 393224 | tf_op jit(solution)/shard_map/ppermute | solution.py:32
  63.9 7.0 %all-to-all-done = f32[16,8,512]{2,1,0:T(8,128)S(1)} async-done(((f32[16,8,512]{2,1,0:T(8,128)}), f32[16,8,512]{2,1,0:T(8,128)S(1)}, u32[]{:S(2)}, u32[]{:S(2)}) %all-to-all-start) | async-done | bytes 262176 | tf_op jit(solution)/shard_map/all_to_all | solution.py:122
  70.9 0.8 collective-permute-done.1
  71.7 0.9 broadcast_in_dim.8
  72.6 9.1 %all-to-all-start.1 = ((f32[32,8,512]{2,1,0:T(8,128)}), f32[32,8,512]{2,1,0:T(8,128)S(1)}, u32[]{:S(2)}, u32[]{:S(2)}) async-start(f32[32,8,512]{2,1,0:T(8,128)} %broadcast_in_dim.8), calls=%async_computation.1 | async-start | bytes 1048576 | tf_op jit(solution)/shard_map/all_to_all | solution.py:50
  81.8 12.7 %all-to-all-done.1 = f32[32,8,512]{2,1,0:T(8,128)S(1)} async-done(((f32[32,8,512]{2,1,0:T(8,128)}), f32[32,8,512]{2,1,0:T(8,128)S(1)}, u32[]{:S(2)}, u32[]{:S(2)}) %all-to-all-start.1) | async-done | bytes 524320 | tf_op jit(solution)/shard_map/all_to_all | solution.py:50
  94.5 0.3 fusion.9
  94.8 0.3 convolution_add_fusion.1
  95.2 0.4 abs_reduce_fusion
  95.9 31.9 %all-gather.7 = f16[2176,512]{1,0:T(8,128)(2,1)S(1)} all-gather(f16[272,512]{1,0:T(8,128)(2,1)S(1)} %pad_maximum_fusion), channel_id=3, replica_groups=mesh['zl'=4,'x'=4,'c'=2,'zh'=2,'y'=8] {'y'}, dimensions={0}, use_global_device_ids=true | all-gather | bytes 2506752 | tf_op jit(solution)/shard_map/all_gather | solution.py:134
  127.8 1.7 fusion.3
  129.5 0.3 copy-done
  129.8 2.4 %shard_map.77 = f32[256,896]{1,0:T(8,128)S(1)} custom-call(s32[1]{0:T(128)} %bitcast.6.core, bf16[4,4,128,896]{3,2,1,0:T(8,128)(2,1)S(1)} %bitcast.32, bf16[8,256,512]{2,1,0:T(8,128)(2,1)S(1)} %get-tuple-element.27.high, bf16[8,256,512]{2,1,0:T(8,128)(2,1)S(1)} %get-tuple-element.26.low), custom_call_target="tpu_custom_call" | custom-call | flops 1879048192 | bytes 8388608 | tf_op jit(solution)/shard_map/pallas_call | solution.py:99
  132.1 10.6 %collective-permute-start.2 = (f32[256,896]{1,0:T(8,128)S(1)}, f32[256,896]{1,0:T(8,128)S(1)}, u32[]{:S(2)}, u32[]{:S(2)}) collective-permute-start(f32[256,896]{1,0:T(8,128)S(1)} %shard_map.77), channel_id=1, source_target_pairs={{0,16},{1,17},{2,18},{3,19},{4,20},{5,21},{6,22},{7,23},{8,24},{9,... | collective-permute-start | bytes 2752520 | tf_op jit(solution)/shard_map/ppermute | solution.py:32
  142.8 2.4 %shard_map.76 = f32[256,896]{1,0:T(8,128)S(1)} custom-call(s32[1]{0:T(128)} %bitcast.core, bf16[4,4,128,896]{3,2,1,0:T(8,128)(2,1)S(1)} %bitcast.33, bf16[8,256,512]{2,1,0:T(8,128)(2,1)S(1)} %get-tuple-element.27.high, bf16[8,256,512]{2,1,0:T(8,128)(2,1)S(1)} %get-tuple-element.26.low), custom_call_target="tpu_custom_call" | custom-call | flops 1879048192 | bytes 8388608 | tf_op jit(solution)/shard_map/pallas_call | solution.py:99
  145.4 16.6 %all_to_all.20 = f32[64,1,128]{2,1,0:T(1,128)S(1)} all-to-all(f32[64,1,128]{2,1,0:T(1,128)S(1)} %broadcast_in_dim.10), channel_id=1, replica_groups=mesh['zl'=4,'x'=4,'c'=2,'zh'=2,'y'=8] {'x','c','y'}, dimensions={0} | all-to-all | bytes 65536 | tf_op jit(solution)/shard_map/all_to_all | solution.py:50
  162.0 8.9 %all_to_all.21 = f32[8,1,128]{2,1,0:T(1,128)S(1)} all-to-all(f32[8,1,128]{2,1,0:T(1,128)S(1)} %broadcast_in_dim.11), channel_id=1, replica_groups=mesh['zl'=4,'x'=4,'c'=2,'zh'=2,'y'=8] {'zh','zl'}, dimensions={0} | all-to-all | bytes 8192 | tf_op jit(solution)/shard_map/all_to_all | solution.py:50
  170.9 0.6 reduce_sum.48
  172.2 1.6 divide_convert_fusion
  (23 shorter events, 0.7 us)
Async XLA Ops:
  7.2 120.6 %all-gather.6.cloned.1.call-start = ((), (), s32[]{:S(2)}) async-start(), calls=%async_computation.4 | async-start | bytes 4587520 | tf_op jit(solution)/shard_map/all_gather | solution.py:119
  7.2 50.3 %collective-permute-start = (bf16[128,512]{1,0:T(8,128)(2,1)}, bf16[128,512]{1,0:T(8,128)(2,1)S(1)}, u32[]{:S(2)}, u32[]{:S(2)}) collective-permute-start(bf16[128,512]{1,0:T(8,128)(2,1)} %param.5), channel_id=1, source_target_pairs={{0,0},{1,32},{2,64},{3,96},{4,128},{5,160},{6,192},{7,224},{8,256}... | collective-permute-start | bytes 393224 | tf_op jit(solution)/shard_map/ppermute | solution.py:32
  58.5 12.4 %all-to-all-start = ((f32[16,8,512]{2,1,0:T(8,128)}), f32[16,8,512]{2,1,0:T(8,128)S(1)}, u32[]{:S(2)}, u32[]{:S(2)}) async-start(f32[16,8,512]{2,1,0:T(8,128)} %convolution_bitcast_fusion), calls=%async_computation | async-start | bytes 524288 | tf_op jit(solution)/shard_map/all_to_all | solution.py:122
  62.0 9.7 %collective-permute-start.1 = (bf16[128,512]{1,0:T(8,128)(2,1)S(1)}, bf16[128,512]{1,0:T(8,128)(2,1)S(1)}, u32[]{:S(2)}, u32[]{:S(2)}) collective-permute-start(bf16[128,512]{1,0:T(8,128)(2,1)S(1)} %collective-permute-done), channel_id=1, source_target_pairs={{0,8},{1,9},{2,10},{3,11},{4,12},{5,13},{6,14},{7,15},{8,0},{9,1},... | collective-permute-start | bytes 393224 | tf_op jit(solution)/shard_map/ppermute | solution.py:32
  72.6 21.9 %all-to-all-start.1 = ((f32[32,8,512]{2,1,0:T(8,128)}), f32[32,8,512]{2,1,0:T(8,128)S(1)}, u32[]{:S(2)}, u32[]{:S(2)}) async-start(f32[32,8,512]{2,1,0:T(8,128)} %broadcast_in_dim.8), calls=%async_computation.1 | async-start | bytes 1048576 | tf_op jit(solution)/shard_map/all_to_all | solution.py:50
  127.7 2.0 %copy-start = (bf16[16,128,896]{2,1,0:T(8,128)(2,1)S(1)}, bf16[16,128,896]{2,1,0:T(8,128)(2,1)}, u32[]{:S(2)}) copy-start(bf16[16,128,896]{2,1,0:T(8,128)(2,1)} %all-gather.6.cloned.1.call-done) | copy-start | bytes 11010052
  132.1 13.1 %collective-permute-start.2 = (f32[256,896]{1,0:T(8,128)S(1)}, f32[256,896]{1,0:T(8,128)S(1)}, u32[]{:S(2)}, u32[]{:S(2)}) collective-permute-start(f32[256,896]{1,0:T(8,128)S(1)} %shard_map.77), channel_id=1, source_target_pairs={{0,16},{1,17},{2,18},{3,19},{4,20},{5,21},{6,22},{7,23},{8,24},{9,... | collective-permute-start | bytes 2752520 | tf_op jit(solution)/shard_map/ppermute | solution.py:32
  142.8 29.4 %copy-start.1 = (f32[256,896]{1,0:T(8,128)S(1)}, f32[256,896]{1,0:T(8,128)}, u32[]{:S(2)}) copy-start(f32[256,896]{1,0:T(8,128)} %param.9) | copy-start | bytes 2752516
  142.8 29.4 %copy-start.2 = (f32[256,896]{1,0:T(8,128)S(1)}, f32[256,896]{1,0:T(8,128)}, u32[]{:S(2)}) copy-start(f32[256,896]{1,0:T(8,128)} %param.8) | copy-start | bytes 2752516
Sparse Core Ops, SparseCore 0:
  57.7 56.9 all-gather.5

commit v5 on v4

--- a/solution.py
+++ b/solution.py
@@ -33,16 +33,19 @@
 
 
 def transpose_place(zl, x, c, zh, y):
-    j = Y * zh + y
-    return j // X, j % X, c, zl // 2, 2 * x + zl % 2
+    return 2 * zh + y // 4, y % 4, c, zl // 2, 4 * (zl % 2) + x
+
+
+def swap_x_y(zl, x, c, zh, y):
+    return zl, y % 4, c, zh, 4 * (y // 4) + x
+
+
+def swap_y_z(zl, x, c, zh, y):
+    return 2 * zh + y // 4, x, c, zl // 2, 4 * (zl % 2) + y % 4
 
 
 def other_core(value):
     return move(value, lambda zl, x, c, zh, y: (zl, x, 1 - c, zh, y))
-
-
-def other_half(value):
-    return move(value, lambda zl, x, c, zh, y: (zl, x, c, 1 - zh, y))
 
 
 def spread(value, axes, n):
@@ -71,8 +74,8 @@
 
 
 def decode(blocks):
-    coded = blocks[:, :256].astype(f32)
-    scale = blocks[:, 256:257].astype(f32) * (2.0**6 / 29.0)
+    coded = blocks[:, :128].astype(f32)
+    scale = blocks[:, 128:129].astype(f32) * (2.0**6 / 29.0)
     size = jnp.log2(jnp.abs(coded)) * scale + 14.0 * scale
     return parts(jnp.where(coded < 0, -size, size), 2)
 
@@ -81,11 +84,12 @@
     rows = pl.ds(pl.multiple_of(core[0] * 256, 256), 256)
     value = None
     for y in range(Y):
-        tokens = [g_ref[y // 2, 2 * zh + y % 2] for zh in range(ZH)]
+        tokens = [g_ref[y % X, 2 * zh + y // X] for zh in range(ZH)]
         tokens = jnp.concatenate(tokens, axis=0)
         for block in (high, low):
+            pair = [block[ZH * y + zh, :, rows] for zh in range(ZH)]
             term = lax.dot_general(
-                block[y, :, rows],
+                jnp.concatenate(pair, axis=0),
                 tokens,
                 (((0,), (0,)), ((), ())),
                 preferred_element_type=f32,
@@ -109,29 +113,29 @@
 
 
 def on_device(features, output_grads, basis, moment_one, moment_two):
-    c, zh, y = lax.axis_index("c"), lax.axis_index("zh"), lax.axis_index("y")
-    own = move(features, transpose_place)
+    c = lax.axis_index("c")
+    direct = move(features[:64], transpose_place)
+    around = move(move(features[64:], swap_x_y), swap_y_z)
+    own = jnp.concatenate([direct, around])
     basis_rows = lax.all_gather(basis, "c", axis=0, tiled=True)
 
-    shard, basis_rows = lax.optimization_barrier((output_grads, basis_rows))
+    shard, own = lax.optimization_barrier((output_grads, own))
     column = lax.all_gather(shard, "zl", axis=0)
-    column, own = lax.optimization_barrier((column, own))
-    g = lax.all_gather(column, "x", axis=0)
-    far = other_half(own)
     partial = jnp.dot(own, basis_rows, preferred_element_type=f32)
     pieces = lax.all_to_all(partial.reshape(16, 8, 512), Q, 0, 0, tiled=True)
-    summed, own, far = lax.optimization_barrier((jnp.sum(pieces, axis=0), own, far))
-    both = jnp.concatenate([jnp.where(zh == 0, own, far), jnp.where(zh == 0, far, own)])
-    coded = spread(summed, ("zh",) + Q, 32).reshape(256, 512)
+    column, pieces = lax.optimization_barrier((column, pieces))
+    g = lax.all_gather(column, "x", axis=0)
+    coded = spread(jnp.sum(pieces, axis=0), Q, 16).reshape(128, 512)
     away = sum(
         lax.dot_general(
             p, basis_rows, (((1,), (1,)), ((), ())), preferred_element_type=f32
         )
         for p in parts(coded, 3)
     )
-    kept = code(both.astype(f32) - away)
+    kept = code(own.astype(f32) - away)
 
-    blocks = lax.all_gather(kept, "y", axis=0)
+    pair = lax.all_gather(kept, "zh", axis=0)
+    blocks = lax.all_gather(pair, "y", axis=0).reshape(Y * ZH, 144, 512)
     blocks, g = lax.optimization_barrier((blocks, g))
 
     high, low = decode(blocks)

time: 181 us -> 174 us (0.961)
  starting transfers between devices: 26.8 us -> 45.9 us
  blocking collectives: 106 us -> 90.8 us
  waiting for transfers between devices: 20.5 us -> 8.86 us
    all_to_all x1, starting transfers between devices: 3.53 us -> 25.6 us  [on_device(): pieces = lax.all_to_all(partial.reshape(16, 8, 512), Q, 0, 0, tiled=True)]
    all_gather x1, blocking collectives: 39.9 us -> 20.5 us  [on_device(): column = lax.all_gather(shard, 'zl', axis=0)]
    all_to_all x1, waiting for transfers between devices: 6.97 us -> 0.01 us  [on_device(): pieces = lax.all_to_all(partial.reshape(16, 8, 512), Q, 0, 0, tiled=True)]
    all_gather x1 -> x2, blocking collectives: 31.9 us -> 36.4 us  [the longest x1 26.6 us: on_device(): blocks = lax.all_gather(pair, 'y', axis=0).reshape(Y * ZH, 144, 512)]
    all_to_all x1, starting transfers between devices: 9.13 us -> 5.03 us  [spread(): return lax.all_to_all(copies, axes, 0, 0, tiled=True)]
    all_to_all x1, waiting for transfers between devices: 12.7 us -> 8.82 us  [spread(): return lax.all_to_all(copies, axes, 0, 0, tiled=True)]
    ppermute x3 -> x4, starting transfers between devices: 14.1 us -> 15.3 us  [move(): return lax.ppermute(value, AXES, pairs)]
  transfers between devices with their start and end apart: 6 -> 7, of which waited for: 3 -> 1; matrix products, arithmetic and copies ran while one was open for 2% -> 1% of each run, Pallas kernels for 1% -> 1%
where the time goes in v5:
time: 174 us; the launch traced here: 173 us
  blocking collectives  90.8 us (52%)
  starting transfers between devices  45.9 us (26%)
  between operations  14.9 us (9%)
  waiting for transfers between devices  8.86 us (5%)
  Pallas kernels  4.76 us (3%)
  other arithmetic  4.44 us (3%)
  matrix products  1.87 us (1%)
  local copies, waits for them, and re-layouts  1.86 us (1%)
    all_gather x1, blocking collectives, on_device(): blocks = lax.all_gather(pair, 'y', axis=0).reshape(Y * ZH, 144, 512)  26.6 us
    all_to_all x1, starting transfers between devices, on_device(): pieces = lax.all_to_all(partial.reshape(16, 8, 512), Q, 0, 0, tiled=True)  25.6 us
    all_to_all x2, blocking collectives, spread(): return lax.all_to_all(copies, axes, 0, 0, tiled=True)  24.9 us
    all_gather x1, blocking collectives, on_device(): column = lax.all_gather(shard, 'zl', axis=0)  20.5 us
    ppermute x4, starting transfers between devices, move(): return lax.ppermute(value, AXES, pairs)  15.3 us
    all_gather x1, blocking collectives, on_device(): pair = lax.all_gather(kept, 'zh', axis=0)  9.82 us
    all_gather x1, blocking collectives, on_device(): basis_rows = lax.all_gather(basis, 'c', axis=0, tiled=True)  8.9 us
    all_to_all x1, waiting for transfers between devices, spread(): return lax.all_to_all(copies, axes, 0, 0, tiled=True)  8.82 us
  transfers between devices with their start and end apart: 7, of which 1 were waited for; matrix products, arithmetic and copies ran while one was open for 1% of the time, Pallas kernels for 1%

profile of v5, /device:TPU:1, one launch (start us, length us, event | category | flops | bytes accessed | tf_op | source)
XLA Modules:
  0.0 173.4 jit_solution(11379339250050951347)
XLA Ops:
  7.2 0.9 fusion.13
  8.0 0.7 collective-permute-start.1
  8.7 0.7 collective-permute-start
  9.4 0.7 collective-permute-start.2
  10.1 8.9 %all_gather.29 = bf16[512,512]{1,0:T(8,128)(2,1)S(1)} all-gather(bf16[256,512]{1,0:T(8,128)(2,1)} %param.7), channel_id=1, replica_groups=mesh['zl'=4,'x'=4,'c'=2,'zh'=2,'y'=8] {'c'}, dimensions={0}, use_global_device_ids=true | all-gather | bytes 786432 | tf_op jit(solution)/shard_map/all_gather | solution.py:120
  19.0 0.9 convolution_bitcast_fusion
  19.9 25.6 %all-to-all-start = ((f32[16,8,512]{2,1,0:T(8,128)}), f32[16,8,512]{2,1,0:T(8,128)S(1)}, u32[]{:S(2)}, u32[]{:S(2)}) async-start(f32[16,8,512]{2,1,0:T(8,128)} %convolution_bitcast_fusion), calls=%async_computation | async-start | bytes 524288 | tf_op jit(solution)/shard_map/all_to_all | solution.py:125
  45.6 20.5 %all-gather = bf16[512,896]{1,0:T(8,128)(2,1)} all-gather(bf16[128,896]{1,0:T(8,128)(2,1)} %param.6), channel_id=2, replica_groups=mesh['zl'=4,'x'=4,'c'=2,'zh'=2,'y'=8] {'zl'}, dimensions={0}, use_global_device_ids=true | all-gather | bytes 1146880 | tf_op jit(solution)/shard_map/all_gather | solution.py:123
  66.1 0.7 broadcast_in_dim.8
  66.9 5.0 %all-to-all-start.1 = ((f32[16,8,512]{2,1,0:T(8,128)}), f32[16,8,512]{2,1,0:T(8,128)S(1)}, u32[]{:S(2)}, u32[]{:S(2)}) async-start(f32[16,8,512]{2,1,0:T(8,128)} %broadcast_in_dim.8), calls=%async_computation.1 | async-start | bytes 524288 | tf_op jit(solution)/shard_map/all_to_all | solution.py:53
  71.9 8.8 %all-to-all-done.1 = f32[16,8,512]{2,1,0:T(8,128)S(1)} async-done(((f32[16,8,512]{2,1,0:T(8,128)}), f32[16,8,512]{2,1,0:T(8,128)S(1)}, u32[]{:S(2)}, u32[]{:S(2)}) %all-to-all-start.1) | async-done | bytes 262176 | tf_op jit(solution)/shard_map/all_to_all | solution.py:53
  80.7 0.3 fusion.9
  81.0 0.3 convolution_add_fusion.1
  81.3 0.3 abs_reduce_fusion
  81.9 9.8 %all-gather.1 = f16[288,512]{1,0:T(8,128)(2,1)S(1)} all-gather(f16[144,512]{1,0:T(8,128)(2,1)S(1)} %pad_maximum_fusion), channel_id=3, replica_groups=mesh['zl'=4,'x'=4,'c'=2,'zh'=2,'y'=8] {'zh'}, dimensions={0}, use_global_device_ids=true | all-gather | bytes 442368 | tf_op jit(solution)/shard_map/all_gather | solution.py:137
  91.7 26.6 %all-gather.8 = f16[16,144,512]{2,1,0:T(8,128)(2,1)S(1)} all-gather(f16[2,144,512]{2,1,0:T(8,128)(2,1)S(1)} %bitcast.35), channel_id=4, replica_groups=mesh['zl'=4,'x'=4,'c'=2,'zh'=2,'y'=8] {'y'}, dimensions={0}, use_global_device_ids=true | all-gather | bytes 2654208 | tf_op jit(solution)/shard_map/all_gather | solution.py:138
  118.4 1.8 %fusion.3 = (bf16[16,128,512]{2,1,0:T(8,128)(2,1)S(1)}, bf16[16,128,512]{2,1,0:T(8,128)(2,1)S(1)}) fusion(f32[16,512]{1,0:T(8,128)S(1)} %get-tuple-element.30, f32[16,512]{1,0:T(8,128)S(1)} %get-tuple-element.31, f16[16,144,512]{2,1,0:T(8,128)(2,1)S(1)} %all-gather.8), kind=kLoop, calls=%fused_computation.8 | loop fusion | flops 11534336 | bytes 6356992 | tf_op jit(solution)/shard_map/convert_element_type | solution.py:62
  120.3 2.4 %shard_map.77 = f32[256,896]{1,0:T(8,128)S(1)} custom-call(s32[1]{0:T(128)} %bitcast.6.core, bf16[4,4,128,896]{3,2,1,0:T(8,128)(2,1)S(1)} %bitcast.32, bf16[16,128,512]{2,1,0:T(8,128)(2,1)S(1)} %get-tuple-element.21.high, bf16[16,128,512]{2,1,0:T(8,128)(2,1)S(1)} %get-tuple-element.20.low), custom_call_target="tpu_custom_call" | custom-call | flops 1879048192 | bytes 8388608 | tf_op jit(solution)/shard_map/pallas_call | solution.py:103
  122.7 13.3 %collective-permute-start.3 = (f32[256,896]{1,0:T(8,128)S(1)}, f32[256,896]{1,0:T(8,128)S(1)}, u32[]{:S(2)}, u32[]{:S(2)}) collective-permute-start(f32[256,896]{1,0:T(8,128)S(1)} %shard_map.77), channel_id=1, source_target_pairs={{0,16},{1,17},{2,18},{3,19},{4,20},{5,21},{6,22},{7,23},{8,24},{9,... | collective-permute-start | bytes 2752520 | tf_op jit(solution)/shard_map/ppermute | solution.py:32
  136.0 2.4 %shard_map.76 = f32[256,896]{1,0:T(8,128)S(1)} custom-call(s32[1]{0:T(128)} %bitcast.core, bf16[4,4,128,896]{3,2,1,0:T(8,128)(2,1)S(1)} %bitcast.33, bf16[16,128,512]{2,1,0:T(8,128)(2,1)S(1)} %get-tuple-element.21.high, bf16[16,128,512]{2,1,0:T(8,128)(2,1)S(1)} %get-tuple-element.20.low), custom_call_target="tpu_custom_call" | custom-call | flops 1879048192 | bytes 8388608 | tf_op jit(solution)/shard_map/pallas_call | solution.py:103
  138.6 14.5 %all_to_all.20 = f32[64,1,128]{2,1,0:T(1,128)S(1)} all-to-all(f32[64,1,128]{2,1,0:T(1,128)S(1)} %broadcast_in_dim.10), channel_id=1, replica_groups=mesh['zl'=4,'x'=4,'c'=2,'zh'=2,'y'=8] {'x','c','y'}, dimensions={0} | all-to-all | bytes 65536 | tf_op jit(solution)/shard_map/all_to_all | solution.py:53
  153.1 10.4 %all_to_all.21 = f32[8,1,128]{2,1,0:T(1,128)S(1)} all-to-all(f32[8,1,128]{2,1,0:T(1,128)S(1)} %broadcast_in_dim.11), channel_id=1, replica_groups=mesh['zl'=4,'x'=4,'c'=2,'zh'=2,'y'=8] {'zh','zl'}, dimensions={0} | all-to-all | bytes 8192 | tf_op jit(solution)/shard_map/all_to_all | solution.py:53
  163.6 0.6 reduce_sum.48
  164.9 1.6 divide_convert_fusion
  (27 shorter events, 0.8 us)
Async XLA Ops:
  8.0 1.3 collective-permute-start.1
  8.7 10.3 %collective-permute-start = (bf16[64,512]{1,0:T(8,128)(2,1)S(1)}, bf16[64,512]{1,0:T(8,128)(2,1)S(1)}, u32[]{:S(2)}, u32[]{:S(2)}) collective-permute-start(bf16[64,512]{1,0:T(8,128)(2,1)S(1)} %get-tuple-element.24), channel_id=1, source_target_pairs={{0,0},{1,32},{2,64},{3,96},{4,128},{5,160},{6,192},{7,224},{8,256}... | collective-permute-start | bytes 196616 | tf_op jit(solution)/shard_map/ppermute | solution.py:32
  9.4 9.6 %collective-permute-start.2 = (bf16[64,512]{1,0:T(8,128)(2,1)S(1)}, bf16[64,512]{1,0:T(8,128)(2,1)S(1)}, u32[]{:S(2)}, u32[]{:S(2)}) collective-permute-start(bf16[64,512]{1,0:T(8,128)(2,1)S(1)} %collective-permute-done.1), channel_id=1, source_target_pairs={{0,0},{1,1},{2,2},{3,3},{4,128},{5,129},{6,130},{7,131},{8,256},{9... | collective-permute-start | bytes 196616 | tf_op jit(solution)/shard_map/ppermute | solution.py:32
  19.9 46.1 %all-to-all-start = ((f32[16,8,512]{2,1,0:T(8,128)}), f32[16,8,512]{2,1,0:T(8,128)S(1)}, u32[]{:S(2)}, u32[]{:S(2)}) async-start(f32[16,8,512]{2,1,0:T(8,128)} %convolution_bitcast_fusion), calls=%async_computation | async-start | bytes 524288 | tf_op jit(solution)/shard_map/all_to_all | solution.py:125
  45.5 72.8 %all-gather.7.cloned.1.call-start = ((), (), s32[]{:S(2)}) async-start(), calls=%async_computation.4 | async-start | bytes 4587520 | tf_op jit(solution)/shard_map/all_gather | solution.py:127
  66.9 13.9 %all-to-all-start.1 = ((f32[16,8,512]{2,1,0:T(8,128)}), f32[16,8,512]{2,1,0:T(8,128)S(1)}, u32[]{:S(2)}, u32[]{:S(2)}) async-start(f32[16,8,512]{2,1,0:T(8,128)} %broadcast_in_dim.8), calls=%async_computation.1 | async-start | bytes 524288 | tf_op jit(solution)/shard_map/all_to_all | solution.py:53
  118.3 2.0 %copy-start = (bf16[16,128,896]{2,1,0:T(8,128)(2,1)S(1)}, bf16[16,128,896]{2,1,0:T(8,128)(2,1)}, u32[]{:S(2)}) copy-start(bf16[16,128,896]{2,1,0:T(8,128)(2,1)} %all-gather.7.cloned.1.call-done) | copy-start | bytes 11010052
  122.7 15.7 %collective-permute-start.3 = (f32[256,896]{1,0:T(8,128)S(1)}, f32[256,896]{1,0:T(8,128)S(1)}, u32[]{:S(2)}, u32[]{:S(2)}) collective-permute-start(f32[256,896]{1,0:T(8,128)S(1)} %shard_map.77), channel_id=1, source_target_pairs={{0,16},{1,17},{2,18},{3,19},{4,20},{5,21},{6,22},{7,23},{8,24},{9,... | collective-permute-start | bytes 2752520 | tf_op jit(solution)/shard_map/ppermute | solution.py:32
  136.0 28.9 %copy-start.1 = (f32[256,896]{1,0:T(8,128)S(1)}, f32[256,896]{1,0:T(8,128)}, u32[]{:S(2)}) copy-start(f32[256,896]{1,0:T(8,128)} %param.9) | copy-start | bytes 2752516
  136.0 28.9 %copy-start.2 = (f32[256,896]{1,0:T(8,128)S(1)}, f32[256,896]{1,0:T(8,128)}, u32[]{:S(2)}) copy-start(f32[256,896]{1,0:T(8,128)} %param.8) | copy-start | bytes 2752516
Sparse Core Ops, SparseCore 0:
  66.2 49.8 all-gather.6

commit v6 on v5

--- a/solution.py
+++ b/solution.py
@@ -68,15 +68,15 @@
     scale = jnp.where(scale * 2.0**6 < largest, scale * (1 + 2.0**-9), scale)
     scale = lax.reduce_precision(scale, 5, 10)
     share = value / (scale * 2.0**6)
-    size = jnp.exp2(29.0 * jnp.abs(share) - 14.0)
+    size = jnp.exp2(28.0 * jnp.abs(share) - 13.0)
     coded = jnp.where(share < 0, -size, size).astype(f16)
-    return jnp.concatenate([coded, jnp.broadcast_to(scale, (16, 512)).astype(f16)])
+    return jnp.concatenate([coded, jnp.broadcast_to(scale, (8, 512)).astype(f16)])
 
 
 def decode(blocks):
     coded = blocks[:, :128].astype(f32)
-    scale = blocks[:, 128:129].astype(f32) * (2.0**6 / 29.0)
-    size = jnp.log2(jnp.abs(coded)) * scale + 14.0 * scale
+    scale = blocks[:, 128:129].astype(f32) * (2.0**6 / 28.0)
+    size = jnp.log2(jnp.abs(coded)) * scale + 13.0 * scale
     return parts(jnp.where(coded < 0, -size, size), 2)
 
 
@@ -135,7 +135,7 @@
     kept = code(own.astype(f32) - away)
 
     pair = lax.all_gather(kept, "zh", axis=0)
-    blocks = lax.all_gather(pair, "y", axis=0).reshape(Y * ZH, 144, 512)
+    blocks = lax.all_gather(pair, "y", axis=0).reshape(Y * ZH, 136, 512)
     blocks, g = lax.optimization_barrier((blocks, g))
 
     high, low = decode(blocks)

time: 174 us -> 173 us (level)
  no operation moved by 1% of the time
where the time goes in v6:
time: 173 us
  blocking collectives  90.3 us (52%)
  starting transfers between devices  45.8 us (26%)
  between operations  14.9 us (9%)
  waiting for transfers between devices  8.86 us (5%)
  Pallas kernels  4.76 us (3%)
  other arithmetic  4.44 us (3%)
  matrix products  1.87 us (1%)
  local copies, waits for them, and re-layouts  1.86 us (1%)
    all_gather x1, blocking collectives, on_device(): blocks = lax.all_gather(pair, 'y', axis=0).reshape(Y * ZH, 136, 512)  26.3 us
    all_to_all x1, starting transfers between devices, on_device(): pieces = lax.all_to_all(partial.reshape(16, 8, 512), Q, 0, 0, tiled=True)  25.6 us
    all_to_all x2, blocking collectives, spread(): return lax.all_to_all(copies, axes, 0, 0, tiled=True)  24.9 us
    all_gather x1, blocking collectives, on_device(): column = lax.all_gather(shard, 'zl', axis=0)  20.5 us
    ppermute x4, starting transfers between devices, move(): return lax.ppermute(value, AXES, pairs)  15.2 us
    all_gather x1, blocking collectives, on_device(): pair = lax.all_gather(kept, 'zh', axis=0)  9.64 us
    all_gather x1, blocking collectives, on_device(): basis_rows = lax.all_gather(basis, 'c', axis=0, tiled=True)  8.9 us
    all_to_all x1, waiting for transfers between devices, spread(): return lax.all_to_all(copies, axes, 0, 0, tiled=True)  8.82 us
  transfers between devices with their start and end apart: 7, of which 1 were waited for; matrix products, arithmetic and copies ran while one was open for 1% of the time, Pallas kernels for 1%

profile of v6, /device:TPU:1, one launch (start us, length us, event | category | flops | bytes accessed | tf_op | source)
XLA Modules:
  0.0 172.8 jit_solution(6247204830944215837)
XLA Ops:
  7.2 0.9 fusion.13
  8.0 0.7 collective-permute-start.1
  8.7 0.7 collective-permute-start
  9.4 0.7 collective-permute-start.2
  10.1 8.9 %all_gather.29 = bf16[512,512]{1,0:T(8,128)(2,1)S(1)} all-gather(bf16[256,512]{1,0:T(8,128)(2,1)} %param.7), channel_id=1, replica_groups=mesh['zl'=4,'x'=4,'c'=2,'zh'=2,'y'=8] {'c'}, dimensions={0}, use_global_device_ids=true | all-gather | bytes 786432 | tf_op jit(solution)/shard_map/all_gather | solution.py:120
  19.0 0.9 convolution_bitcast_fusion
  19.9 25.6 %all-to-all-start = ((f32[16,8,512]{2,1,0:T(8,128)}), f32[16,8,512]{2,1,0:T(8,128)S(1)}, u32[]{:S(2)}, u32[]{:S(2)}) async-start(f32[16,8,512]{2,1,0:T(8,128)} %convolution_bitcast_fusion), calls=%async_computation | async-start | bytes 524288 | tf_op jit(solution)/shard_map/all_to_all | solution.py:125
  45.6 20.5 %all-gather = bf16[512,896]{1,0:T(8,128)(2,1)} all-gather(bf16[128,896]{1,0:T(8,128)(2,1)} %param.6), channel_id=2, replica_groups=mesh['zl'=4,'x'=4,'c'=2,'zh'=2,'y'=8] {'zl'}, dimensions={0}, use_global_device_ids=true | all-gather | bytes 1146880 | tf_op jit(solution)/shard_map/all_gather | solution.py:123
  66.1 0.7 broadcast_in_dim.8
  66.9 5.0 %all-to-all-start.1 = ((f32[16,8,512]{2,1,0:T(8,128)}), f32[16,8,512]{2,1,0:T(8,128)S(1)}, u32[]{:S(2)}, u32[]{:S(2)}) async-start(f32[16,8,512]{2,1,0:T(8,128)} %broadcast_in_dim.8), calls=%async_computation.1 | async-start | bytes 524288 | tf_op jit(solution)/shard_map/all_to_all | solution.py:53
  71.9 8.8 %all-to-all-done.1 = f32[16,8,512]{2,1,0:T(8,128)S(1)} async-done(((f32[16,8,512]{2,1,0:T(8,128)}), f32[16,8,512]{2,1,0:T(8,128)S(1)}, u32[]{:S(2)}, u32[]{:S(2)}) %all-to-all-start.1) | async-done | bytes 262176 | tf_op jit(solution)/shard_map/all_to_all | solution.py:53
  80.7 0.3 fusion.9
  81.0 0.3 convolution_add_fusion.1
  81.3 0.3 abs_reduce_fusion
  81.9 9.6 %all-gather.1 = f16[272,512]{1,0:T(8,128)(2,1)S(1)} all-gather(f16[136,512]{1,0:T(8,128)(2,1)S(1)} %pad_maximum_fusion), channel_id=3, replica_groups=mesh['zl'=4,'x'=4,'c'=2,'zh'=2,'y'=8] {'zh'}, dimensions={0}, use_global_device_ids=true | all-gather | bytes 417792 | tf_op jit(solution)/shard_map/all_gather | solution.py:137
  91.5 26.3 %all-gather.8 = f16[16,136,512]{2,1,0:T(8,128)(2,1)S(1)} all-gather(f16[2,136,512]{2,1,0:T(8,128)(2,1)S(1)} %bitcast.35), channel_id=4, replica_groups=mesh['zl'=4,'x'=4,'c'=2,'zh'=2,'y'=8] {'y'}, dimensions={0}, use_global_device_ids=true | all-gather | bytes 2506752 | tf_op jit(solution)/shard_map/all_gather | solution.py:138
  117.9 1.8 %fusion.3 = (bf16[16,128,512]{2,1,0:T(8,128)(2,1)S(1)}, bf16[16,128,512]{2,1,0:T(8,128)(2,1)S(1)}) fusion(f32[16,512]{1,0:T(8,128)S(1)} %get-tuple-element.30, f32[16,512]{1,0:T(8,128)S(1)} %get-tuple-element.31, f16[16,136,512]{2,1,0:T(8,128)(2,1)S(1)} %all-gather.8), kind=kLoop, calls=%fused_computation.8 | loop fusion | flops 11534336 | bytes 6356992 | tf_op jit(solution)/shard_map/convert_element_type | solution.py:62
  119.9 2.4 %shard_map.77 = f32[256,896]{1,0:T(8,128)S(1)} custom-call(s32[1]{0:T(128)} %bitcast.6.core, bf16[4,4,128,896]{3,2,1,0:T(8,128)(2,1)S(1)} %bitcast.32, bf16[16,128,512]{2,1,0:T(8,128)(2,1)S(1)} %get-tuple-element.21.high, bf16[16,128,512]{2,1,0:T(8,128)(2,1)S(1)} %get-tuple-element.20.low), custom_call_target="tpu_custom_call" | custom-call | flops 1879048192 | bytes 8388608 | tf_op jit(solution)/shard_map/pallas_call | solution.py:103
  122.3 13.2 %collective-permute-start.3 = (f32[256,896]{1,0:T(8,128)S(1)}, f32[256,896]{1,0:T(8,128)S(1)}, u32[]{:S(2)}, u32[]{:S(2)}) collective-permute-start(f32[256,896]{1,0:T(8,128)S(1)} %shard_map.77), channel_id=1, source_target_pairs={{0,16},{1,17},{2,18},{3,19},{4,20},{5,21},{6,22},{7,23},{8,24},{9,... | collective-permute-start | bytes 2752520 | tf_op jit(solution)/shard_map/ppermute | solution.py:32
  135.5 2.4 %shard_map.76 = f32[256,896]{1,0:T(8,128)S(1)} custom-call(s32[1]{0:T(128)} %bitcast.core, bf16[4,4,128,896]{3,2,1,0:T(8,128)(2,1)S(1)} %bitcast.33, bf16[16,128,512]{2,1,0:T(8,128)(2,1)S(1)} %get-tuple-element.21.high, bf16[16,128,512]{2,1,0:T(8,128)(2,1)S(1)} %get-tuple-element.20.low), custom_call_target="tpu_custom_call" | custom-call | flops 1879048192 | bytes 8388608 | tf_op jit(solution)/shard_map/pallas_call | solution.py:103
  138.1 14.3 %all_to_all.20 = f32[64,1,128]{2,1,0:T(1,128)S(1)} all-to-all(f32[64,1,128]{2,1,0:T(1,128)S(1)} %broadcast_in_dim.10), channel_id=1, replica_groups=mesh['zl'=4,'x'=4,'c'=2,'zh'=2,'y'=8] {'x','c','y'}, dimensions={0} | all-to-all | bytes 65536 | tf_op jit(solution)/shard_map/all_to_all | solution.py:53
  152.5 10.6 %all_to_all.21 = f32[8,1,128]{2,1,0:T(1,128)S(1)} all-to-all(f32[8,1,128]{2,1,0:T(1,128)S(1)} %broadcast_in_dim.11), channel_id=1, replica_groups=mesh['zl'=4,'x'=4,'c'=2,'zh'=2,'y'=8] {'zh','zl'}, dimensions={0} | all-to-all | bytes 8192 | tf_op jit(solution)/shard_map/all_to_all | solution.py:53
  163.0 0.6 reduce_sum.48
  164.3 1.6 divide_convert_fusion
  (27 shorter events, 0.8 us)
Async XLA Ops:
  8.0 1.3 collective-permute-start.1
  8.7 10.3 %collective-permute-start = (bf16[64,512]{1,0:T(8,128)(2,1)S(1)}, bf16[64,512]{1,0:T(8,128)(2,1)S(1)}, u32[]{:S(2)}, u32[]{:S(2)}) collective-permute-start(bf16[64,512]{1,0:T(8,128)(2,1)S(1)} %get-tuple-element.24), channel_id=1, source_target_pairs={{0,0},{1,32},{2,64},{3,96},{4,128},{5,160},{6,192},{7,224},{8,256}... | collective-permute-start | bytes 196616 | tf_op jit(solution)/shard_map/ppermute | solution.py:32
  9.4 9.6 %collective-permute-start.2 = (bf16[64,512]{1,0:T(8,128)(2,1)S(1)}, bf16[64,512]{1,0:T(8,128)(2,1)S(1)}, u32[]{:S(2)}, u32[]{:S(2)}) collective-permute-start(bf16[64,512]{1,0:T(8,128)(2,1)S(1)} %collective-permute-done.1), channel_id=1, source_target_pairs={{0,0},{1,1},{2,2},{3,3},{4,128},{5,129},{6,130},{7,131},{8,256},{9... | collective-permute-start | bytes 196616 | tf_op jit(solution)/shard_map/ppermute | solution.py:32
  19.9 46.1 %all-to-all-start = ((f32[16,8,512]{2,1,0:T(8,128)}), f32[16,8,512]{2,1,0:T(8,128)S(1)}, u32[]{:S(2)}, u32[]{:S(2)}) async-start(f32[16,8,512]{2,1,0:T(8,128)} %convolution_bitcast_fusion), calls=%async_computation | async-start | bytes 524288 | tf_op jit(solution)/shard_map/all_to_all | solution.py:125
  45.5 72.3 %all-gather.7.cloned.1.call-start = ((), (), s32[]{:S(2)}) async-start(), calls=%async_computation.4 | async-start | bytes 4587520 | tf_op jit(solution)/shard_map/all_gather | solution.py:127
  66.9 13.9 %all-to-all-start.1 = ((f32[16,8,512]{2,1,0:T(8,128)}), f32[16,8,512]{2,1,0:T(8,128)S(1)}, u32[]{:S(2)}, u32[]{:S(2)}) async-start(f32[16,8,512]{2,1,0:T(8,128)} %broadcast_in_dim.8), calls=%async_computation.1 | async-start | bytes 524288 | tf_op jit(solution)/shard_map/all_to_all | solution.py:53
  117.8 2.0 %copy-start = (bf16[16,128,896]{2,1,0:T(8,128)(2,1)S(1)}, bf16[16,128,896]{2,1,0:T(8,128)(2,1)}, u32[]{:S(2)}) copy-start(bf16[16,128,896]{2,1,0:T(8,128)(2,1)} %all-gather.7.cloned.1.call-done) | copy-start | bytes 11010052
  122.3 15.7 %collective-permute-start.3 = (f32[256,896]{1,0:T(8,128)S(1)}, f32[256,896]{1,0:T(8,128)S(1)}, u32[]{:S(2)}, u32[]{:S(2)}) collective-permute-start(f32[256,896]{1,0:T(8,128)S(1)} %shard_map.77), channel_id=1, source_target_pairs={{0,16},{1,17},{2,18},{3,19},{4,20},{5,21},{6,22},{7,23},{8,24},{9,... | collective-permute-start | bytes 2752520 | tf_op jit(solution)/shard_map/ppermute | solution.py:32
  135.5 28.8 %copy-start.1 = (f32[256,896]{1,0:T(8,128)S(1)}, f32[256,896]{1,0:T(8,128)}, u32[]{:S(2)}) copy-start(f32[256,896]{1,0:T(8,128)} %param.9) | copy-start | bytes 2752516
  135.5 28.8 %copy-start.2 = (f32[256,896]{1,0:T(8,128)S(1)}, f32[256,896]{1,0:T(8,128)}, u32[]{:S(2)}) copy-start(f32[256,896]{1,0:T(8,128)} %param.8) | copy-start | bytes 2752516
Sparse Core Ops, SparseCore 0:
  66.2 49.8 all-gather.6

commit v7 on v6

--- a/solution.py
+++ b/solution.py
@@ -82,20 +82,18 @@
 
 def grad_kernel(core, g_ref, high, low, out):
     rows = pl.ds(pl.multiple_of(core[0] * 256, 256), 256)
-    value = None
-    for y in range(Y):
-        tokens = [g_ref[y % X, 2 * zh + y // X] for zh in range(ZH)]
-        tokens = jnp.concatenate(tokens, axis=0)
-        for block in (high, low):
-            pair = [block[ZH * y + zh, :, rows] for zh in range(ZH)]
-            term = lax.dot_general(
-                jnp.concatenate(pair, axis=0),
-                tokens,
-                (((0,), (0,)), ((), ())),
-                preferred_element_type=f32,
-            )
-            value = term if value is None else value + term
-    out[...] = value
+    tokens = [g_ref[y % X, 2 * zh + y // X] for y in range(Y) for zh in range(ZH)]
+    tokens = jnp.concatenate(tokens, axis=0)
+    terms = [
+        lax.dot_general(
+            block[:, :, rows].reshape(2048, 256),
+            tokens,
+            (((0,), (0,)), ((), ())),
+            preferred_element_type=f32,
+        )
+        for block in (high, low)
+    ]
+    out[...] = terms[0] + terms[1]
 
 
 def call(kernel, core, g, given):

time: 173 us -> 173 us (level)
  no operation moved by 1% of the time
where the time goes in v7:
time: 173 us
  blocking collectives  90.3 us (52%)
  starting transfers between devices  45.9 us (27%)
  between operations  14.9 us (9%)
  waiting for transfers between devices  8.86 us (5%)
  Pallas kernels  4.79 us (3%)
  other arithmetic  4.44 us (3%)
  matrix products  1.87 us (1%)
  local copies, waits for them, and re-layouts  1.86 us (1%)
    all_gather x1, blocking collectives, on_device(): blocks = lax.all_gather(pair, 'y', axis=0).reshape(Y * ZH, 136, 512)  26.3 us
    all_to_all x1, starting transfers between devices, on_device(): pieces = lax.all_to_all(partial.reshape(16, 8, 512), Q, 0, 0, tiled=True)  25.6 us
    all_to_all x2, blocking collectives, spread(): return lax.all_to_all(copies, axes, 0, 0, tiled=True)  24.9 us
    all_gather x1, blocking collectives, on_device(): column = lax.all_gather(shard, 'zl', axis=0)  20.5 us
    ppermute x4, starting transfers between devices, move(): return lax.ppermute(value, AXES, pairs)  15.2 us
    all_gather x1, blocking collectives, on_device(): pair = lax.all_gather(kept, 'zh', axis=0)  9.64 us
    all_gather x1, blocking collectives, on_device(): basis_rows = lax.all_gather(basis, 'c', axis=0, tiled=True)  8.9 us
    all_to_all x1, waiting for transfers between devices, spread(): return lax.all_to_all(copies, axes, 0, 0, tiled=True)  8.82 us
  transfers between devices with their start and end apart: 7, of which 1 were waited for; matrix products, arithmetic and copies ran while one was open for 1% of the time, Pallas kernels for 1%

profile of v7, /device:TPU:1, one launch (start us, length us, event | category | flops | bytes accessed | tf_op | source)
XLA Modules:
  0.0 172.9 jit_solution(15146869771669744021)
XLA Ops:
  7.2 0.9 fusion.13
  8.0 0.7 collective-permute-start.1
  8.7 0.7 collective-permute-start
  9.4 0.7 collective-permute-start.2
  10.1 8.9 %all_gather.29 = bf16[512,512]{1,0:T(8,128)(2,1)S(1)} all-gather(bf16[256,512]{1,0:T(8,128)(2,1)} %param.7), channel_id=1, replica_groups=mesh['zl'=4,'x'=4,'c'=2,'zh'=2,'y'=8] {'c'}, dimensions={0}, use_global_device_ids=true | all-gather | bytes 786432 | tf_op jit(solution)/shard_map/all_gather | solution.py:118
  19.0 0.9 convolution_bitcast_fusion
  19.9 25.6 %all-to-all-start = ((f32[16,8,512]{2,1,0:T(8,128)}), f32[16,8,512]{2,1,0:T(8,128)S(1)}, u32[]{:S(2)}, u32[]{:S(2)}) async-start(f32[16,8,512]{2,1,0:T(8,128)} %convolution_bitcast_fusion), calls=%async_computation | async-start | bytes 524288 | tf_op jit(solution)/shard_map/all_to_all | solution.py:123
  45.6 20.5 %all-gather = bf16[512,896]{1,0:T(8,128)(2,1)} all-gather(bf16[128,896]{1,0:T(8,128)(2,1)} %param.6), channel_id=2, replica_groups=mesh['zl'=4,'x'=4,'c'=2,'zh'=2,'y'=8] {'zl'}, dimensions={0}, use_global_device_ids=true | all-gather | bytes 1146880 | tf_op jit(solution)/shard_map/all_gather | solution.py:121
  66.1 0.7 broadcast_in_dim.8
  66.9 5.0 %all-to-all-start.1 = ((f32[16,8,512]{2,1,0:T(8,128)}), f32[16,8,512]{2,1,0:T(8,128)S(1)}, u32[]{:S(2)}, u32[]{:S(2)}) async-start(f32[16,8,512]{2,1,0:T(8,128)} %broadcast_in_dim.8), calls=%async_computation.1 | async-start | bytes 524288 | tf_op jit(solution)/shard_map/all_to_all | solution.py:53
  71.9 8.8 %all-to-all-done.1 = f32[16,8,512]{2,1,0:T(8,128)S(1)} async-done(((f32[16,8,512]{2,1,0:T(8,128)}), f32[16,8,512]{2,1,0:T(8,128)S(1)}, u32[]{:S(2)}, u32[]{:S(2)}) %all-to-all-start.1) | async-done | bytes 262176 | tf_op jit(solution)/shard_map/all_to_all | solution.py:53
  80.7 0.3 fusion.9
  81.0 0.3 convolution_add_fusion.1
  81.3 0.3 abs_reduce_fusion
  81.9 9.6 %all-gather.1 = f16[272,512]{1,0:T(8,128)(2,1)S(1)} all-gather(f16[136,512]{1,0:T(8,128)(2,1)S(1)} %pad_maximum_fusion), channel_id=3, replica_groups=mesh['zl'=4,'x'=4,'c'=2,'zh'=2,'y'=8] {'zh'}, dimensions={0}, use_global_device_ids=true | all-gather | bytes 417792 | tf_op jit(solution)/shard_map/all_gather | solution.py:135
  91.5 26.3 %all-gather.8 = f16[16,136,512]{2,1,0:T(8,128)(2,1)S(1)} all-gather(f16[2,136,512]{2,1,0:T(8,128)(2,1)S(1)} %bitcast.35), channel_id=4, replica_groups=mesh['zl'=4,'x'=4,'c'=2,'zh'=2,'y'=8] {'y'}, dimensions={0}, use_global_device_ids=true | all-gather | bytes 2506752 | tf_op jit(solution)/shard_map/all_gather | solution.py:136
  117.9 1.8 %fusion.3 = (bf16[16,128,512]{2,1,0:T(8,128)(2,1)S(1)}, bf16[16,128,512]{2,1,0:T(8,128)(2,1)S(1)}) fusion(f32[16,512]{1,0:T(8,128)S(1)} %get-tuple-element.30, f32[16,512]{1,0:T(8,128)S(1)} %get-tuple-element.31, f16[16,136,512]{2,1,0:T(8,128)(2,1)S(1)} %all-gather.8), kind=kLoop, calls=%fused_computation.8 | loop fusion | flops 11534336 | bytes 6356992 | tf_op jit(solution)/shard_map/convert_element_type | solution.py:62
  119.9 2.4 %shard_map.77 = f32[256,896]{1,0:T(8,128)S(1)} custom-call(s32[1]{0:T(128)} %bitcast.6.core, bf16[4,4,128,896]{3,2,1,0:T(8,128)(2,1)S(1)} %bitcast.32, bf16[16,128,512]{2,1,0:T(8,128)(2,1)S(1)} %get-tuple-element.21.high, bf16[16,128,512]{2,1,0:T(8,128)(2,1)S(1)} %get-tuple-element.20.low), custom_call_target="tpu_custom_call" | custom-call | flops 1879048192 | bytes 8388608 | tf_op jit(solution)/shard_map/pallas_call | solution.py:101
  122.3 13.3 %collective-permute-start.3 = (f32[256,896]{1,0:T(8,128)S(1)}, f32[256,896]{1,0:T(8,128)S(1)}, u32[]{:S(2)}, u32[]{:S(2)}) collective-permute-start(f32[256,896]{1,0:T(8,128)S(1)} %shard_map.77), channel_id=1, source_target_pairs={{0,16},{1,17},{2,18},{3,19},{4,20},{5,21},{6,22},{7,23},{8,24},{9,... | collective-permute-start | bytes 2752520 | tf_op jit(solution)/shard_map/ppermute | solution.py:32
  135.5 2.4 %shard_map.76 = f32[256,896]{1,0:T(8,128)S(1)} custom-call(s32[1]{0:T(128)} %bitcast.core, bf16[4,4,128,896]{3,2,1,0:T(8,128)(2,1)S(1)} %bitcast.33, bf16[16,128,512]{2,1,0:T(8,128)(2,1)S(1)} %get-tuple-element.21.high, bf16[16,128,512]{2,1,0:T(8,128)(2,1)S(1)} %get-tuple-element.20.low), custom_call_target="tpu_custom_call" | custom-call | flops 1879048192 | bytes 8388608 | tf_op jit(solution)/shard_map/pallas_call | solution.py:101
  138.1 14.3 %all_to_all.20 = f32[64,1,128]{2,1,0:T(1,128)S(1)} all-to-all(f32[64,1,128]{2,1,0:T(1,128)S(1)} %broadcast_in_dim.10), channel_id=1, replica_groups=mesh['zl'=4,'x'=4,'c'=2,'zh'=2,'y'=8] {'x','c','y'}, dimensions={0} | all-to-all | bytes 65536 | tf_op jit(solution)/shard_map/all_to_all | solution.py:53
  152.5 10.6 %all_to_all.21 = f32[8,1,128]{2,1,0:T(1,128)S(1)} all-to-all(f32[8,1,128]{2,1,0:T(1,128)S(1)} %broadcast_in_dim.11), channel_id=1, replica_groups=mesh['zl'=4,'x'=4,'c'=2,'zh'=2,'y'=8] {'zh','zl'}, dimensions={0} | all-to-all | bytes 8192 | tf_op jit(solution)/shard_map/all_to_all | solution.py:53
  163.1 0.6 reduce_sum.48
  164.4 1.6 divide_convert_fusion
  (27 shorter events, 0.8 us)
Async XLA Ops:
  8.0 1.3 collective-permute-start.1
  8.7 10.3 %collective-permute-start = (bf16[64,512]{1,0:T(8,128)(2,1)S(1)}, bf16[64,512]{1,0:T(8,128)(2,1)S(1)}, u32[]{:S(2)}, u32[]{:S(2)}) collective-permute-start(bf16[64,512]{1,0:T(8,128)(2,1)S(1)} %get-tuple-element.24), channel_id=1, source_target_pairs={{0,0},{1,32},{2,64},{3,96},{4,128},{5,160},{6,192},{7,224},{8,256}... | collective-permute-start | bytes 196616 | tf_op jit(solution)/shard_map/ppermute | solution.py:32
  9.4 9.6 %collective-permute-start.2 = (bf16[64,512]{1,0:T(8,128)(2,1)S(1)}, bf16[64,512]{1,0:T(8,128)(2,1)S(1)}, u32[]{:S(2)}, u32[]{:S(2)}) collective-permute-start(bf16[64,512]{1,0:T(8,128)(2,1)S(1)} %collective-permute-done.1), channel_id=1, source_target_pairs={{0,0},{1,1},{2,2},{3,3},{4,128},{5,129},{6,130},{7,131},{8,256},{9... | collective-permute-start | bytes 196616 | tf_op jit(solution)/shard_map/ppermute | solution.py:32
  19.9 46.1 %all-to-all-start = ((f32[16,8,512]{2,1,0:T(8,128)}), f32[16,8,512]{2,1,0:T(8,128)S(1)}, u32[]{:S(2)}, u32[]{:S(2)}) async-start(f32[16,8,512]{2,1,0:T(8,128)} %convolution_bitcast_fusion), calls=%async_computation | async-start | bytes 524288 | tf_op jit(solution)/shard_map/all_to_all | solution.py:123
  45.5 72.3 %all-gather.7.cloned.1.call-start = ((), (), s32[]{:S(2)}) async-start(), calls=%async_computation.4 | async-start | bytes 4587520 | tf_op jit(solution)/shard_map/all_gather | solution.py:125
  66.9 13.9 %all-to-all-start.1 = ((f32[16,8,512]{2,1,0:T(8,128)}), f32[16,8,512]{2,1,0:T(8,128)S(1)}, u32[]{:S(2)}, u32[]{:S(2)}) async-start(f32[16,8,512]{2,1,0:T(8,128)} %broadcast_in_dim.8), calls=%async_computation.1 | async-start | bytes 524288 | tf_op jit(solution)/shard_map/all_to_all | solution.py:53
  117.8 2.0 %copy-start = (bf16[16,128,896]{2,1,0:T(8,128)(2,1)S(1)}, bf16[16,128,896]{2,1,0:T(8,128)(2,1)}, u32[]{:S(2)}) copy-start(bf16[16,128,896]{2,1,0:T(8,128)(2,1)} %all-gather.7.cloned.1.call-done) | copy-start | bytes 11010052
  122.3 15.7 %collective-permute-start.3 = (f32[256,896]{1,0:T(8,128)S(1)}, f32[256,896]{1,0:T(8,128)S(1)}, u32[]{:S(2)}, u32[]{:S(2)}) collective-permute-start(f32[256,896]{1,0:T(8,128)S(1)} %shard_map.77), channel_id=1, source_target_pairs={{0,16},{1,17},{2,18},{3,19},{4,20},{5,21},{6,22},{7,23},{8,24},{9,... | collective-permute-start | bytes 2752520 | tf_op jit(solution)/shard_map/ppermute | solution.py:32
  135.5 28.9 %copy-start.1 = (f32[256,896]{1,0:T(8,128)S(1)}, f32[256,896]{1,0:T(8,128)}, u32[]{:S(2)}) copy-start(f32[256,896]{1,0:T(8,128)} %param.9) | copy-start | bytes 2752516
  135.5 28.9 %copy-start.2 = (f32[256,896]{1,0:T(8,128)S(1)}, f32[256,896]{1,0:T(8,128)}, u32[]{:S(2)}) copy-start(f32[256,896]{1,0:T(8,128)} %param.8) | copy-start | bytes 2752516
Sparse Core Ops, SparseCore 0:
  66.2 49.8 all-gather.6
